TPU v7x, 128 devices: a whole 4x4x4 slice. The times are simulated.
128 devices in a mesh: mp: 8 (over z, x_lo), dp: 16 (over x_hi, y, core).
Axes of the slice: x: 4 (x_hi: 2, x_lo: 2; x = x_hi * 2 + x_lo), y: 4, z: 4, core: 2. Of those that a mesh axis runs over, the one named last changes fastest.
Arguments:
- volume: bfloat16 [16, 64, 64, 2048], P('dp', 'mp'), may hold values from -6 to 6
- kernel_a: bfloat16 [3, 3, 3, 32, 64], replicated, may hold values from -0.21875 to 0.21875
- kernel_b: bfloat16 [3, 3, 3, 64, 128], P(None, None, None, 'mp'), may hold values from -0.15625 to 0.15625
- cotangent: bfloat16 [16, 16, 16, 16, 128], P('dp', None, None, None, 'mp'), may hold values from -6 to 6
Outputs:
- features: bfloat16 [16, 16, 16, 16, 128], P('dp', None, None, None, 'mp')
- grad_a: float32 [3, 3, 3, 32, 64], replicated
- grad_b: float32 [3, 3, 3, 64, 128], P(None, None, None, 'mp')
All inputs are finite; a program needn't handle non-finite values.
Results may differ from a plain program's by a relative error of at most 0.0049.
Values may be sent and summed in bfloat16 or wider, within the bound.
A program may use at most 192 MiB of HBM per device.

v0:
```python
import math

import jax
import jax.numpy as jnp
from jax import lax
from jax.sharding import PartitionSpec as P

GRID = 64


def shifted(array, axis, by):
    size = lax.axis_size(axis)
    pairs = [(i, i + by) for i in range(size) if 0 <= i + by < size]
    return lax.ppermute(array, axis, pairs)


def forward_conv(padded, kernel):
    return lax.conv_general_dilated(
        padded,
        kernel,
        (2, 2, 2),
        "VALID",
        dimension_numbers=("NDHWC", "DHWIO", "NDHWC"),
        preferred_element_type=jnp.float32,
    )


def kernel_grad(padded, grads):
    result = lax.conv_general_dilated(
        padded,
        grads,
        (1, 1, 1),
        "VALID",
        rhs_dilation=(2, 2, 2),
        dimension_numbers=("CDHWN", "IDHWO", "NDHWC"),
        preferred_element_type=jnp.float32,
    )
    return jnp.transpose(result, (1, 2, 3, 0, 4))


def input_grad(grads, kernel, first_low):
    flipped = kernel[::-1, ::-1, ::-1]
    return lax.conv_general_dilated(
        grads,
        flipped,
        (1, 1, 1),
        ((first_low, 2), (1, 2), (1, 2)),
        lhs_dilation=(2, 2, 2),
        dimension_numbers=("NDHWC", "DHWOI", "NDHWC"),
        preferred_element_type=jnp.float32,
    )


def pad_sides(field):
    return jnp.pad(field, ((0, 0), (0, 0), (1, 0), (1, 0), (0, 0)))


def pad_low(field):
    return jnp.pad(field, ((0, 0), (1, 0), (1, 0), (1, 0), (0, 0)))


def shards(volume, kernel_a, kernel_b, cotangent):
    samp_local = volume.shape[0]
    planes = volume.shape[1]
    edge = volume.shape[2]
    in_chan = kernel_a.shape[3]
    field = volume.reshape(samp_local, planes, edge, edge, in_chan)
    below = shifted(field[:, planes - 1 :], "mp", 1)
    padded_x = pad_sides(jnp.concatenate([below, field], axis=1))
    pre = forward_conv(padded_x, kernel_a)
    hidden = jnp.where(pre > 0, pre, 0.3 * pre).astype(jnp.bfloat16)
    grouped = lax.all_to_all(hidden, "mp", split_axis=4, concat_axis=1, tiled=True)
    padded_h = pad_low(grouped)
    partial_out = forward_conv(padded_h, kernel_b)
    features = lax.psum_scatter(partial_out, "mp", scatter_dimension=4, tiled=True).astype(
        jnp.bfloat16
    )
    upstream = lax.all_gather(cotangent, "mp", axis=4, tiled=True)
    local_b = kernel_grad(padded_h, upstream)
    back_group = input_grad(upstream, kernel_b, 1).astype(jnp.bfloat16)
    back = lax.all_to_all(back_group, "mp", split_axis=1, concat_axis=4, tiled=True)
    delta = (back.astype(jnp.float32) * jnp.where(pre > 0, 1.0, 0.3)).astype(jnp.bfloat16)
    local_a = kernel_grad(padded_x, delta)
    total_a = lax.psum(local_a, ("mp", "dp"))
    total_b = lax.psum(local_b, "dp")
    samples_all = samp_local * lax.axis_size("dp")
    grad_a = total_a / math.sqrt(samples_all * (GRID // 2) ** 3)
    grad_b = total_b / math.sqrt(samples_all * (GRID // 4) ** 3)
    return (features, grad_a, grad_b)


def solution(mesh):
    return jax.shard_map(
        shards,
        mesh=mesh,
        in_specs=(
            P("dp", "mp", None, None),
            P(),
            P(None, None, None, "mp", None),
            P("dp", None, None, None, "mp"),
        ),
        out_specs=(P("dp", None, None, None, "mp"), P(), P(None, None, None, "mp", None)),
        check_vma=False,
    )
```

profile of v0, /device:TPU:1, one launch (start us, length us, event | category | flops | bytes accessed | tf_op | source)
XLA Modules:
  0.0 838.3 jit_solution(7763710412680146833)
XLA Ops:
  7.2 4.9 copy.124
  14.2 4.0 collective-permute-start
  18.2 31.5 %copy.127 = bf16[1,8,64,64,32]{4,0,3,2,1:T(2,128)(2,1)} copy(bf16[1,8,64,64,32]{2,4,3,1,0:T(8,128)(2,1)} %bitcast.69) | data formatting | bytes 4194304 | tf_op jit(solution)/shard_map/reshape | solution.py:67
  52.4 58.2 %pad_maximum_fusion = bf16[1,9,64,64,32]{4,0,3,2,1:T(2,128)(2,1)} fusion(bf16[1,8,64,64,32]{4,0,3,2,1:T(2,128)(2,1)} %copy.127, bf16[1,1,64,64,32]{4,0,3,2,1:T(2,128)(2,1)S(1)} %copy.126), kind=kLoop, calls=%fused_computation.4 | loop fusion | flops 1179648 | bytes 4718592 | tf_op jit(solution)/shard_map/concatenate | solution.py:69
  110.6 33.5 %copy.128 = bf16[1,9,64,64,32]{3,4,2,1,0:T(8,128)(2,1)} copy(bf16[1,9,64,64,32]{4,0,3,2,1:T(2,128)(2,1)} %pad_maximum_fusion) | data formatting | bytes 4718592 | tf_op jit(solution)/shard_map/concatenate | solution.py:69
  144.1 9.2 %copy.159 = bf16[9,64,1,64,32]{1,4,3,0,2:T(8,128)(2,1)} copy(bf16[9,64,1,64,32]{3,4,2,1,0:T(8,128)(2,1)} %bitcast.72) | data formatting | bytes 4718592
  153.3 6.1 pad.4.clone
  159.4 15.6 %copy.131 = bf16[9,64,1,8,10,32]{5,3,4,1,0,2:T(8,128)(2,1)} copy(bf16[9,64,1,8,10,32]{1,5,4,3,0,2:T(8,128)(2,1)} %bitcast.67) | data formatting | bytes 5898240 | tf_op jit(solution)/shard_map/conv_general_dilated | solution.py:18
  177.4 12.0 %compare_select_fusion = (f32[4,32,8,5,64]{4,2,3,1,0:T(8,128)}, bf16[4,32,8,5,64]{4,2,3,1,0:T(8,128)(2,1)S(1)}) fusion(pred[8,5]{0,1:T(8,128)(4,1)S(1)} %copy-done.6, bf16[3,3,3,32,64]{4,3,2,1,0:T(8,128)(2,1)S(1)} %copy-done, bf16[9,64,1,7,2,32]{5,3,4,1,0,2:T(8,128)(2,1)S(1)} %slice.12, bf16[9,64,1,8,10,32]{5,3,4,1,0,2:T(8,128)(2,1)} %copy.131), kind=kOutput, calls=%fused_computation.20 | convolution fusion | flops 572915712 | bytes 5541928 | tf_op jit(solution)/shard_map/conv_general_dilated | solution.py:18
  195.8 6.1 all-to-all-start
  202.0 3.9 copy.140
  216.9 3.4 copy.160
  220.4 4.0 pad.6.clone
  224.4 12.8 %copy.138 = bf16[32,32,1,8,6,8]{5,3,4,1,0,2:T(8,128)(2,1)} copy(bf16[32,32,1,8,6,8]{1,5,4,3,0,2:T(8,128)(2,1)} %bitcast.73) | data formatting | bytes 1572864 | tf_op jit(solution)/shard_map/conv_general_dilated | solution.py:18
  240.6 12.3 %broadcast_select_fusion = f32[16,16,8,3,128]{4,2,3,1,0:T(8,128)S(1)} fusion(pred[8,3]{0,1:T(4,128)(4,1)S(1)} %copy-done.7, bf16[3,3,3,8,128]{4,3,2,1,0:T(8,128)(2,1)S(1)} %copy-done.5, bf16[32,32,1,7,2,8]{5,3,4,1,0,2:T(8,128)(2,1)S(1)} %slice.14, bf16[32,32,1,8,6,8]{5,3,4,1,0,2:T(8,128)(2,1)} %copy.138), kind=kOutput, calls=%fused_computation.30 | convolution fusion | flops 329662464 | bytes 4216856 | tf_op jit(solution)/shard_map/conv_general_dilated | solution.py:18
  255.2 23.8 %copy.153 = bf16[1,32,32,32,8]{4,0,3,2,1:T(2,128)(2,1)} copy(bf16[1,32,32,32,8]{3,4,2,1,0:T(8,128)(2,1)S(1)} %bitcast.71) | data formatting | bytes 1048576 | tf_op jit(solution)/shard_map/all_to_all | solution.py:72
  279.0 97.7 %all-gather.2.cloned.1.call-done = bf16[1,16,16,16,128]{3,2,1,0,4:T(8,128)(2,1)} async-done(((bf16[1,16,16,16,16]{3,2,1,0,4:T(8,128)(2,1)}), bf16[1,16,16,16,128]{3,2,1,0,4:T(8,128)(2,1)}) %all-gather.2.cloned.1.call-update) | async-done | bytes 1048592 | tf_op jit(solution)/shard_map/all_gather | solution.py:78
  376.7 10.0 %copy.141 = bf16[1,16,16,16,128]{4,3,2,1,0:T(8,128)(2,1)S(1)} copy(bf16[1,16,16,16,128]{3,2,1,0,4:T(8,128)(2,1)} %all-gather.2.cloned.1.call-done) | data formatting | bytes 2097152 | tf_op jit(solution)/shard_map/all_gather | solution.py:78
  387.9 14.3 %fusion.17 = bf16[32,32,8,6,8]{4,2,3,1,0:T(8,128)(2,1)} fusion(bf16[3,3,3,8,128]{4,3,2,1,0:T(8,128)(2,1)S(1)} %copy-done.5, bf16[16,16,1,7,1,128]{5,3,4,1,0,2:T(8,128)(2,1)S(1)} %slice.16, bf16[16,16,1,8,3,128]{5,3,4,1,0,2:T(8,128)(2,1)S(1)} %copy.144), kind=kOutput, calls=%fused_computation.24 | convolution fusion | flops 332021760 | bytes 2873344 | tf_op jit(solution)/shard_map/conv_general_dilated | solution.py:43
  402.2 13.6 %copy.145 = bf16[32,32,8,6,8]{1,4,3,2,0:T(8,128)(2,1)S(1)} copy(bf16[32,32,8,6,8]{4,2,3,1,0:T(8,128)(2,1)} %fusion.17) | data formatting | bytes 1572864 | tf_op jit(solution)/shard_map/conv_general_dilated | solution.py:43
  419.7 4.9 all-to-all-start.1
  424.6 13.5 %copy.154 = bf16[1,16,16,16,128]{4,0,3,2,1:T(2,128)(2,1)S(1)} copy(bf16[1,16,16,16,128]{3,2,1,0,4:T(8,128)(2,1)} %all-gather.2.cloned.1.call-done) | data formatting | bytes 2097152 | tf_op jit(solution)/shard_map/all_gather | solution.py:78
  438.1 51.8 %fusion.36 = f32[3,3,3,8,128]{4,3,2,1,0:T(8,128)} fusion(bf16[1,32,32,32,8]{4,0,3,2,1:T(2,128)(2,1)} %copy.153, bf16[1,16,16,16,128]{4,0,3,2,1:T(2,128)(2,1)S(1)} %copy.154), kind=kOutput, calls=%fused_computation.46 | convolution fusion | flops 212629504 | bytes 1683456 | tf_op jit(solution)/shard_map/transpose | solution.py:38
  491.3 3.4 copy.147
  494.7 3.5 fusion.12
  498.2 4.1 copy.151
  502.3 46.6 %fusion.35 = f32[3,3,3,32,64]{4,3,2,1,0:T(8,128)} fusion(bf16[1,9,64,64,32]{4,0,3,2,1:T(2,128)(2,1)} %pad_maximum_fusion, bf16[1,4,32,32,64]{4,0,3,2,1:T(2,128)(2,1)} %copy.151), kind=kOutput, calls=%fused_computation.45 | convolution fusion | flops 443596800 | bytes 3104768 | tf_op jit(solution)/shard_map/transpose | solution.py:38
  550.5 14.3 %copy.156 = f32[1,16,16,16,128]{2,3,1,0,4:T(8,128)} copy(f32[1,16,16,16,128]{4,2,3,1,0:T(8,128)} %slice_bitcast_fusion.1) | data formatting | bytes 4194304
  564.8 15.3 %reshape.69 = f32[128,4096]{1,0:T(8,128)} reshape(f32[128,1,16,16,16]{4,3,2,1,0:T(8,128)} %bitcast.66) | data formatting | bytes 4194304
  580.1 45.1 %all-reduce.5.cloned.1.call-done = f32[3,3,3,8,128]{4,3,2,1,0:T(8,128)} async-done(((f32[3,3,3,8,128]{4,3,2,1,0:T(8,128)}), f32[3,3,3,8,128]{4,3,2,1,0:T(8,128)}) %all-reduce.5.cloned.1.call-update) | async-done | bytes 110608 | tf_op jit(solution)/shard_map/psum | solution.py:85
  626.8 147.3 %all-reduce.3.cloned.1.call-done = f32[3,3,3,32,64]{4,3,2,1,0:T(8,128)} async-done(((f32[3,3,3,32,64]{4,3,2,1,0:T(8,128)}), f32[3,3,3,32,64]{4,3,2,1,0:T(8,128)}) %all-reduce.3.cloned.1.call-update) | async-done | bytes 221200 | tf_op jit(solution)/shard_map/psum | solution.py:84
  775.9 51.3 %reduce-scatter.4.cloned.1.call-done = f32[16,4096]{1,0:T(8,128)} async-done(((f32[128,4096]{1,0:T(8,128)}), f32[16,4096]{1,0:T(8,128)}) %reduce-scatter.4.cloned.1.call-update) | async-done | bytes 262160
  (57 shorter events, 46.0 us)
Async XLA Ops:
  7.2 170.2 %copy-start = (bf16[3,3,3,32,64]{4,3,2,1,0:T(8,128)(2,1)S(1)}, bf16[3,3,3,32,64]{4,3,2,1,0:T(8,128)(2,1)}, u32[]{:S(2)}) copy-start(bf16[3,3,3,32,64]{4,3,2,1,0:T(8,128)(2,1)} %param.5) | copy-start | bytes 331780
  14.2 35.5 %collective-permute-start = (bf16[1,1,64,64,32]{3,4,2,1,0:T(8,128)(2,1)S(1)}, bf16[1,1,64,64,32]{3,4,2,1,0:T(8,128)(2,1)S(1)}, u32[]{:S(2)}, u32[]{:S(2)}) collective-permute-start(bf16[1,1,64,64,32]{3,4,2,1,0:T(8,128)(2,1)S(1)} %copy.125), channel_id=1, source_target_pairs={{0,16},{16,32},{32,48},{48,64},{64,80},{80,96},{96,112},{1,17},{17... | collective-permute-start | bytes 786440 | tf_op jit(solution)/shard_map/ppermute | solution.py:14
  175.0 2.4 copy-start.6
  195.8 10.1 %copy-start.3 = (f32[4,32,8,5,64]{4,2,3,1,0:T(8,128)S(1)}, f32[4,32,8,5,64]{4,2,3,1,0:T(8,128)}, u32[]{:S(2)}) copy-start(f32[4,32,8,5,64]{4,2,3,1,0:T(8,128)} %get-tuple-element.18) | copy-start | bytes 3932164
  195.8 15.0 %all-to-all-start = ((bf16[8,2,16384]{2,1,0:T(2,128)(2,1)}), bf16[8,2,16384]{2,1,0:T(2,128)(2,1)S(1)}, u32[]{:S(2)}, u32[]{:S(2)}) async-start(bf16[8,2,16384]{2,1,0:T(2,128)(2,1)} %reshape.71), calls=%async_computation | async-start | bytes 1048576 | tf_op jit(solution)/shard_map/all_to_all | solution.py:72
  202.0 174.8 %all-gather.2.cloned.1.call-start = ((), (), s32[]{:S(2)}) async-start(), calls=%async_computation.3 | async-start | bytes 9437184 | tf_op jit(solution)/shard_map/all_gather | solution.py:78
  237.2 3.4 copy-start.5
  237.2 3.5 copy-start.7
  402.2 13.6 %copy-start.4 = (pred[8,6]{1,0:T(8,128)(4,1)S(1)}, pred[8,6]{1,0:T(8,128)(4,1)}, u32[]{:S(2)}) copy-start(pred[8,6]{1,0:T(8,128)(4,1)} %constant.31) | copy-start | bytes 148
  419.7 70.3 %all-to-all-start.1 = ((bf16[8,2,16384]{2,1,0:T(2,128)(2,1)}), bf16[8,2,16384]{2,1,0:T(2,128)(2,1)S(1)}, u32[]{:S(2)}, u32[]{:S(2)}) async-start(bf16[8,2,16384]{2,1,0:T(2,128)(2,1)} %reshape.73), calls=%async_computation.1 | async-start | bytes 1048576 | tf_op jit(solution)/shard_map/all_to_all | solution.py:81
  424.6 200.6 %all-reduce.5.cloned.1.call-start = ((), (), s32[]{:S(2)}) async-start(), calls=%async_computation.5 | async-start | bytes 221184 | tf_op jit(solution)/shard_map/psum | solution.py:85
  489.9 284.1 %all-reduce.3.cloned.1.call-start = ((), (), s32[]{:S(2)}) async-start(), calls=%async_computation.4 | async-start | bytes 884736 | tf_op jit(solution)/shard_map/psum | solution.py:84
  502.3 46.7 %copy-start.2 = (f32[16,16,8,3,128]{4,1,3,2,0:T(8,128)S(1)}, f32[16,16,8,3,128]{4,1,3,2,0:T(8,128)}, u32[]{:S(2)}) copy-start(f32[16,16,8,3,128]{4,1,3,2,0:T(8,128)} %copy.139) | copy-start | bytes 9437188
  548.9 278.3 %reduce-scatter.4.cloned.1.call-start = ((), (), s32[]{:S(2)}) async-start(), calls=%async_computation.6 | async-start | bytes 2359296
  625.2 206.2 %copy-start.1 = (bf16[3,3,3,32,64]{4,3,2,1,0:T(8,128)(2,1)S(1)}, bf16[3,3,3,32,64]{4,3,2,1,0:T(8,128)(2,1)}, u32[]{:S(2)}) copy-start(bf16[3,3,3,32,64]{4,3,2,1,0:T(8,128)(2,1)} %param.5) | copy-start | bytes 331780
Sparse Core Ops, SparseCore 0:
  206.0 170.6 all-gather.1
  490.1 135.0 all-reduce.4
  631.2 142.7 all-reduce.2
  776.3 50.8 reduce-scatter.3
where the time goes:
time: 853 us; the launch traced here: 838 us
  waiting for transfers between devices  343 us (40%)
  local copies, waits for them, and re-layouts  263 us (31%)
  matrix products  137 us (16%)
  other arithmetic  66 us (8%)
  starting transfers between devices  15.2 us (2%)
  between operations  14.4 us (2%)
    psum x1, waiting for transfers between devices, shards(): total_a = lax.psum(local_a, ('mp', 'dp'))  147 us
    transpose x2, matrix products, kernel_grad(): return jnp.transpose(result, (1, 2, 3, 0, 4))  98.3 us
    all_gather x1, waiting for transfers between devices, shards(): upstream = lax.all_gather(cotangent, 'mp', axis=4, tiled=True)  97.7 us
    unnamed x32, local copies, waits for them, and re-layouts  66.3 us
    concatenate x1, other arithmetic, shards(): padded_x = pad_sides(jnp.concatenate([below, field], axis=1))  58.2 us
    unnamed x5, waiting for transfers between devices  51.4 us
    psum x1, waiting for transfers between devices, shards(): total_b = lax.psum(local_b, 'dp')  45.1 us
    concatenate x2, local copies, waits for them, and re-layouts, shards(): padded_x = pad_sides(jnp.concatenate([below, field], axis=1))  39.5 us
  transfers between devices with their start and end apart: 7, of which 5 were waited for; matrix products, arithmetic and copies ran while one was open for 32% of the time, Pallas kernels for 0%

commit v1 on v0

v1 whole, which is shorter than its diff:
```python
import functools
import math

import jax
import jax.numpy as jnp
from jax import lax
from jax.experimental import pallas as pl
from jax.experimental.pallas import tpu as pltpu
from jax.sharding import PartitionSpec as P

BF = jnp.bfloat16
F32 = jnp.float32
MESH = pl.DeviceIdType.MESH
SLABS = 8
CORES = 2
GROUP = SLABS * CORES
ROWS_B = 112
ROWS_A = 32


def dot(lhs, rhs):
    return jnp.dot(lhs, rhs, preferred_element_type=F32)


def dot_nt(lhs, rhs):
    return lax.dot_general(lhs, rhs, (((1,), (1,)), ((), ())), preferred_element_type=F32)


def dot_tn(lhs, rhs):
    return lax.dot_general(lhs, rhs, (((0,), (0,)), ((), ())), preferred_element_type=F32)


def later(tiles):
    zero = jnp.zeros((16, tiles.shape[1]), tiles.dtype)
    return jnp.concatenate([zero, tiles[:-16]], axis=0)


def earlier(tiles):
    zero = jnp.zeros((16, tiles.shape[1]), tiles.dtype)
    return jnp.concatenate([tiles[16:], zero], axis=0)


def row_below(tiles):
    rolled = pltpu.roll(tiles.astype(F32), 1, 0)
    row = lax.broadcasted_iota(jnp.int32, tiles.shape, 0)
    return jnp.where(lax.rem(row, 16) == 0, 0.0, rolled).astype(BF)


def body(
    ring,
    scale_a,
    scale_b,
    x,
    ka,
    kb,
    cot,
    feat,
    ga,
    gb,
    xv,
    xs,
    xt,
    wa,
    pf,
    hs,
    ht,
    ct_loc,
    ct_all,
    kb_all,
    kb_f,
    wb,
    vb,
    cs,
    cc,
    ft,
    fr,
    dd,
    gb_f,
    gb_s,
    gb_1,
    gb_2s,
    gb_2,
    gb_3,
    ga_f,
    ga_s,
    ga_1,
    ga_2s,
    ga_2,
    ga_3,
    x_sem,
    xh_send,
    xh_recv,
    hh_send,
    hh_recv,
    ct_send,
    ct_recv,
    kb_send,
    kb_recv,
    ft_send,
    ft_recv,
    b1_send,
    b1_recv,
    b2_send,
    b2_recv,
    b3_send,
    b3_recv,
    a1_send,
    a1_recv,
    a2_send,
    a2_recv,
    a3_send,
    a3_recv,
):
    mp = lax.axis_index("mp")
    dp = lax.axis_index("dp")
    core = lax.rem(dp, CORES)
    rank = lax.div(dp, CORES)
    me = mp * CORES + core

    def in_group(index):
        return {"mp": lax.div(index, CORES), "dp": rank * CORES + lax.rem(index, CORES)}

    def in_slabs(index):
        return {"mp": index, "dp": dp}

    def in_ring(index):
        return {"mp": mp, "dp": index * CORES + core}

    def others(size, mine, act):
        @pl.loop(1, size)
        def _(step):
            act(lax.rem(mine + step, size))

    def remote(src, dst, send, recv, device):
        return pltpu.make_async_remote_copy(
            src_ref=src, dst_ref=dst, send_sem=send, recv_sem=recv, device_id=device, device_id_type=MESH
        )

    barrier = pltpu.get_barrier_semaphore()
    others(GROUP, me, lambda i: pl.semaphore_signal(barrier, inc=1, device_id=in_group(i), device_id_type=MESH))
    others(ring, rank, lambda i: pl.semaphore_signal(barrier, inc=1, device_id=in_ring(i), device_id_type=MESH))

    def plane_copy(plane):
        return pltpu.make_async_copy(x.at[plane], xv.at[plane + 1], x_sem.at[plane])

    @pl.loop(0, 8)
    def _(step):
        plane_copy(7 - step).start()

    eye = (
        lax.broadcasted_iota(jnp.int32, (16, 16), 0) == lax.broadcasted_iota(jnp.int32, (16, 16), 1)
    ).astype(BF)

    @pl.loop(0, 8)
    def _(pair):
        rows = cot[pl.ds(pl.multiple_of(pair * 512, 512), 512), :]
        ct_loc[:, pl.ds(pl.multiple_of(pair * 512, 512), 512)] = dot_nt(eye, rows).astype(BF)

    ct_loc[:, 4096:4352] = jnp.zeros((16, 256), BF)
    kb_all[mp] = jnp.concatenate([kb[...].astype(F32), jnp.zeros((8, 128), F32)], axis=0).astype(BF)

    pl.semaphore_wait(barrier, GROUP - 1 + ring - 1)

    def x_halo():
        return remote(x.at[7], xv.at[0], xh_send, xh_recv, in_slabs(mp + 1))

    def h_halo():
        return remote(hs.at[4, pl.ds(1, 2)], hs.at[0, pl.ds(1, 2)], hh_send, hh_recv, in_slabs(mp + 1))

    def ct_copy(peer, slot):
        src = ct_loc.at[:, pl.ds(pl.multiple_of(peer * 512, 512), 768)]
        return remote(src, ct_all.at[slot], ct_send.at[peer], ct_recv.at[slot], in_slabs(peer))

    def kb_copy(peer, slot):
        return remote(kb_all.at[mp], kb_all.at[slot], kb_send.at[peer], kb_recv.at[slot], in_slabs(peer))

    def ft_copy(peer, slot):
        return remote(ft.at[peer], fr.at[slot], ft_send.at[peer], ft_recv.at[slot], in_slabs(peer))

    def b1_copy(peer, slot):
        return remote(gb_s.at[peer], gb_1.at[slot], b1_send.at[peer], b1_recv.at[slot], in_group(peer))

    def b2_copy(peer, slot):
        return remote(gb_2s, gb_2.at[slot], b2_send.at[peer], b2_recv.at[slot], in_ring(peer))

    def b3_copy(slot):
        return remote(gb_3.at[core], gb_3.at[slot], b3_send, b3_recv, in_group(mp * CORES + 1 - core))

    def a1_copy(peer, slot):
        return remote(ga_s.at[peer], ga_1.at[slot], a1_send.at[peer], a1_recv.at[slot], in_group(peer))

    def a2_copy(peer, slot):
        return remote(ga_2s, ga_2.at[slot], a2_send.at[peer], a2_recv.at[slot], in_ring(peer))

    def a3_copy(peer, slot):
        return remote(ga_3.at[me], ga_3.at[slot], a3_send.at[peer], a3_recv.at[slot], in_group(peer))

    @pl.when(mp < SLABS - 1)
    def _():
        x_halo().start()

    others(SLABS, mp, lambda i: kb_copy(i, mp).start())
    others(SLABS, mp, lambda i: ct_copy(i, mp).start())
    ct_all[mp] = ct_loc[:, pl.ds(pl.multiple_of(mp * 512, 512), 768)]

    @pl.loop(0, 9)
    def _(ab):
        k0 = ka[ab, 0:32, :]
        k1 = ka[ab, 32:64, :]
        k2 = ka[ab, 64:96, :]
        no = jnp.zeros((32, 64), BF)
        wa[ab, 0:32, :] = jnp.concatenate([k1, no, no, no], axis=1)
        wa[ab, 32:64, :] = jnp.concatenate([k2, k0, no, no], axis=1)
        wa[ab, 64:96, :] = jnp.concatenate([no, k1, no, no], axis=1)
        wa[ab, 96:128, :] = jnp.concatenate([no, k2, k0, no], axis=1)

    pick_row = lax.broadcasted_iota(jnp.int32, (80, 64), 0)
    pick_col = lax.broadcasted_iota(jnp.int32, (80, 64), 1)
    pick = (pick_col == 4 * lax.rem(pick_row, 16) + lax.div(pick_row, 16) - 1).astype(BF)

    def prepare(index):
        rows = dot(pick, xv[index]).astype(BF)
        for s in range(5):
            for q in range(16):
                xs[index, s, q * 16 : q * 16 + 16, :] = rows[s * 16 : s * 16 + 16, q * 128 : q * 128 + 128]

    plane_copy(7).wait()
    prepare(8)

    @pl.loop(0, 4)
    def _(step):
        depth = 3 - step
        plane_copy(2 * depth).wait()
        prepare(2 * depth + 1)

        @pl.when(depth > 0)
        def _():
            plane_copy(2 * depth - 1).wait()

        @pl.when(jnp.logical_and(depth == 0, mp > 0))
        def _():
            x_halo().wait_recv()

        @pl.when(jnp.logical_and(depth == 0, mp == 0))
        def _():
            xv[0] = jnp.zeros((64, 2048), BF)

        prepare(2 * depth)
        weights = wa[...].reshape(9 * 128, 256)
        for rh in range(2):
            parts = [xs[2 * depth + a, 2 * rh + b] for a in range(3) for b in range(3)]
            both = dot(jnp.concatenate(parts, axis=1), weights)
            pre = both[:, :128] + later(both[:, 128:])
            pf[depth, rh] = pre
            hidden = jnp.where(pre > 0, pre, 0.3 * pre).astype(BF)
            hs[depth + 1, rh + 1] = hidden
            if rh == 1:
                hs[depth + 1, 0] = row_below(hidden)

        @pl.when(jnp.logical_and(depth == 3, mp < SLABS - 1))
        def _():
            h_halo().start()

    @pl.loop(0, 9)
    def _(index):
        for s in range(5):
            xt[index, s] = xs[index, s].T

    others(SLABS, mp, lambda i: kb_copy(i, i).wait_recv())

    @pl.loop(0, 8)
    def _(e):
        kb_f[e] = kb_all[e].astype(F32)

    @pl.loop(0, 9)
    def _(ab):
        k0, k1, k2 = [
            kb_f[:, pl.ds(pl.multiple_of(ab * 24 + c * 8, 8), 8), :].reshape(64, 128) for c in range(3)
        ]
        this = jnp.concatenate([k1, k2], axis=0)
        last = jnp.concatenate([jnp.zeros((64, 128), F32), k0], axis=0)
        wb[ab] = jnp.concatenate([this, last], axis=1).astype(BF)
        vb[ab] = jnp.concatenate([this.T, last.T], axis=1).astype(BF)

    others(SLABS, mp, lambda i: ct_copy(i, i).wait_recv())
    order_row = lax.broadcasted_iota(jnp.int32, (512, 256), 0)
    order_col = lax.broadcasted_iota(jnp.int32, (512, 256), 1)
    order_pos = lax.rem(order_row, 256)
    order = (
        order_col == (lax.rem(order_pos, 16) + lax.div(order_row, 256)) * 16 + lax.div(order_pos, 16)
    ).astype(BF)
    for p in range(3):
        lanes = ct_all[:, :, p * 256 : p * 256 + 256].reshape(128, 256)
        both = dot_nt(order, lanes).astype(BF)
        cs[p, 0] = both[:256]
        cs[p, 1] = both[256:]
        if p < 2:
            cc[p] = jnp.concatenate([both[:256], earlier(both[:256])], axis=1)

    @pl.when(mp > 0)
    def _():
        h_halo().wait_recv()

    @pl.when(mp == 0)
    def _():
        hs[0] = jnp.zeros((3, 256, 128), BF)

    hs[0, 0] = row_below(hs[0, 2])

    @pl.loop(0, 5)
    def _(index):
        for b in range(3):
            ht[index, b] = hs[index, b].T

    @pl.loop(0, 2)
    def _(depth):
        parts = [hs[2 * depth + a, b] for a in range(3) for b in range(3)]
        both = dot(jnp.concatenate(parts, axis=1), wb[...].reshape(9 * 128, 256))
        out = (both[:, :128] + later(both[:, 128:])).astype(BF)
        turned = dot_tn(out, order[:256]).astype(BF)
        ft[:, :, pl.ds(pl.multiple_of(depth * 256, 256), 256)] = turned.reshape(8, 16, 256)

    others(SLABS, mp, lambda i: ft_copy(i, mp).start())
    fr[mp] = ft[mp]

    @pl.loop(0, 3)
    def _(a):
        lhs = jnp.concatenate(
            [jnp.concatenate([ht[2 * p + a, b] for b in range(3)], axis=0) for p in range(2)], axis=1
        )
        acc = dot(lhs, cc[...].reshape(512, 256))
        for b in range(3):
            block = acc[b * 128 : b * 128 + 128]
            pieces = (block[64:, 128:], block[:64, :128], block[64:, :128])
            for c in range(3):
                start = pl.multiple_of(a * 72 + b * 24 + c * 8, 8)
                gb_f[:, pl.ds(start, 8), :] = pieces[c].reshape(8, 8, 128)

    gb_f[:, 216:224, :] = jnp.zeros((8, 8, 128), F32)

    @pl.loop(0, 8)
    def _(e):
        for k in range(CORES):
            gb_s[e * CORES + k] = gb_f[e, k * ROWS_B : (k + 1) * ROWS_B, :].astype(BF)

    others(GROUP, me, lambda i: b1_copy(i, me).start())
    gb_1[me] = gb_s[me]

    @pl.loop(0, 2)
    def _(depth):
        for rd in range(2):
            for rh in range(2):
                along = [(1, 0)] if rd == 0 else [(2, 0), (0, 1)]
                down = [(1, 0)] if rh == 0 else [(2, 0), (0, 1)]
                lhs = [cs[depth + ahead, low] for _, ahead in along for _, low in down]
                rhs = [vb[a * 3 + b] for a, _ in along for b, _ in down]
                both = dot(jnp.concatenate(lhs, axis=1), jnp.concatenate(rhs, axis=0))
                back = (both[:, :128] + earlier(both[:, 128:])).astype(BF).astype(F32)
                slope = jnp.where(pf[2 * depth + rd, rh] > 0, 1.0, 0.3)
                delta = back * slope
                dd[2 * depth + rd, rh] = jnp.concatenate([delta, earlier(delta)], axis=1).astype(BF)

    others(GROUP, me, lambda i: b1_copy(i, i).wait_recv())
    gb_2s[...] = jnp.sum(gb_1[...].astype(F32), axis=0)
    others(ring, rank, lambda i: b2_copy(i, rank).start())
    gb_2[rank] = gb_2s[...]

    lane = lax.broadcasted_iota(jnp.int32, (16, 128), 1)

    @pl.loop(0, 3)
    def _(a):
        lhs = jnp.concatenate(
            [
                jnp.concatenate([xt[2 * depth + a, 2 * rh + b] for b in range(3)], axis=0)
                for depth in range(4)
                for rh in range(2)
            ],
            axis=1,
        )
        acc = dot(lhs, dd[...].reshape(2048, 256))
        for b in range(3):
            this = acc[b * 128 : b * 128 + 128, :128]
            last = acc[b * 128 + 96 : b * 128 + 128, 128:]
            turned = pltpu.roll(this, 64, 1)
            sums = (last + turned[32:64], this[0:32] + turned[64:96], this[32:64] + turned[96:128])
            for c in range(3):
                packed = jnp.where(lane < 64, sums[c][:16], pltpu.roll(sums[c][16:], 64, 1))
                ga_f[pl.ds(pl.multiple_of(a * 144 + b * 48 + c * 16, 16), 16), :] = packed

    ga_f[432:512, :] = jnp.zeros((80, 128), F32)
    ga_s[...] = ga_f[...].reshape(GROUP, ROWS_A, 128).astype(BF)
    others(GROUP, me, lambda i: a1_copy(i, me).start())
    ga_1[me] = ga_s[me]

    others(ring, rank, lambda i: b2_copy(i, i).wait_recv())
    gb_3[core] = jnp.sum(gb_2[...], axis=0) * scale_b
    b3_copy(core).start()

    others(GROUP, me, lambda i: a1_copy(i, i).wait_recv())
    ga_2s[...] = jnp.sum(ga_1[...].astype(F32), axis=0)
    others(ring, rank, lambda i: a2_copy(i, rank).start())
    ga_2[rank] = ga_2s[...]

    others(SLABS, mp, lambda i: ft_copy(i, i).wait_recv())
    for e in range(SLABS):
        feat[:, e * 512 : e * 512 + 512] = fr[e]

    b3_copy(1 - core).wait_recv()
    gb[0:ROWS_B, :] = gb_3[0]
    gb[ROWS_B:216, :] = gb_3[1, : 216 - ROWS_B, :]

    others(ring, rank, lambda i: a2_copy(i, i).wait_recv())
    ga_3[me] = jnp.sum(ga_2[...], axis=0) * scale_a
    others(GROUP, me, lambda i: a3_copy(i, me).start())

    @pl.when(mp < SLABS - 1)
    def _():
        x_halo().wait_send()
        h_halo().wait_send()

    others(SLABS, mp, lambda i: kb_copy(i, mp).wait_send())
    others(SLABS, mp, lambda i: ct_copy(i, mp).wait_send())
    others(SLABS, mp, lambda i: ft_copy(i, mp).wait_send())
    others(GROUP, me, lambda i: b1_copy(i, me).wait_send())
    others(ring, rank, lambda i: b2_copy(i, rank).wait_send())
    b3_copy(core).wait_send()
    others(GROUP, me, lambda i: a1_copy(i, me).wait_send())
    others(ring, rank, lambda i: a2_copy(i, rank).wait_send())

    others(GROUP, me, lambda i: a3_copy(i, i).wait_recv())
    whole = ga_3[...].reshape(GROUP * ROWS_A, 128)[:432].reshape(27, 16, 128)
    ga[:, 0:16, :] = whole[:, :, :64]
    ga[:, 16:32, :] = whole[:, :, 64:]
    others(GROUP, me, lambda i: a3_copy(i, me).wait_send())


def shards(ring, samples, volume, kernel_a, kernel_b, cotangent):
    scale_a = 1.0 / math.sqrt(samples * 32**3)
    scale_b = 1.0 / math.sqrt(samples * 16**3)
    vmem = pltpu.VMEM
    dma = pltpu.SemaphoreType.DMA
    scratch = [
        vmem((9, 64, 2048), BF),
        vmem((9, 5, 256, 128), BF),
        vmem((9, 5, 128, 256), BF),
        vmem((9, 128, 256), BF),
        vmem((4, 2, 256, 128), F32),
        vmem((5, 3, 256, 128), BF),
        vmem((5, 3, 128, 256), BF),
        vmem((16, 4352), BF),
        vmem((8, 16, 768), BF),
        vmem((8, 224, 128), BF),
        vmem((8, 224, 128), F32),
        vmem((9, 128, 256), BF),
        vmem((9, 128, 256), BF),
        vmem((3, 2, 256, 128), BF),
        vmem((2, 256, 256), BF),
        vmem((8, 16, 512), BF),
        vmem((8, 16, 512), BF),
        vmem((4, 2, 256, 256), BF),
        vmem((8, 224, 128), F32),
        vmem((GROUP, ROWS_B, 128), BF),
        vmem((GROUP, ROWS_B, 128), BF),
        vmem((ROWS_B, 128), F32),
        vmem((ring, ROWS_B, 128), F32),
        vmem((CORES, ROWS_B, 128), F32),
        vmem((512, 128), F32),
        vmem((GROUP, ROWS_A, 128), BF),
        vmem((GROUP, ROWS_A, 128), BF),
        vmem((ROWS_A, 128), F32),
        vmem((ring, ROWS_A, 128), F32),
        vmem((GROUP, ROWS_A, 128), F32),
        dma((8,)),
        dma,
        dma,
        dma,
        dma,
        dma((8,)),
        dma((8,)),
        dma((8,)),
        dma((8,)),
        dma((8,)),
        dma((8,)),
        dma((GROUP,)),
        dma((GROUP,)),
        dma((ring,)),
        dma((ring,)),
        dma,
        dma,
        dma((GROUP,)),
        dma((GROUP,)),
        dma((ring,)),
        dma((ring,)),
        dma((GROUP,)),
        dma((GROUP,)),
    ]
    in_vmem = pl.BlockSpec(memory_space=pltpu.VMEM)
    feat, ga, gb = pl.pallas_call(
        functools.partial(body, ring, scale_a, scale_b),
        out_shape=(
            jax.ShapeDtypeStruct((16, 4096), BF),
            jax.ShapeDtypeStruct((27, 32, 64), F32),
            jax.ShapeDtypeStruct((216, 128), F32),
        ),
        in_specs=[pl.BlockSpec(memory_space=pl.ANY), in_vmem, in_vmem, in_vmem],
        out_specs=(in_vmem, in_vmem, in_vmem),
        scratch_shapes=scratch,
        compiler_params=pltpu.CompilerParams(
            collective_id=0, has_side_effects=True, vmem_limit_bytes=48 * 1024 * 1024
        ),
        cost_estimate=pl.CostEstimate(flops=1600000000, bytes_accessed=4000000, transcendentals=0),
    )(
        volume.reshape(8, 64, 2048),
        kernel_a.reshape(9, 96, 64),
        kernel_b.reshape(216, 128),
        cotangent.reshape(4096, 16),
    )
    features = feat.T.reshape(1, 16, 16, 16, 16)
    return (features, ga.reshape(3, 3, 3, 32, 64), gb.reshape(3, 3, 3, 8, 128))


def solution(mesh):
    ring = mesh.shape["dp"] // CORES
    return jax.shard_map(
        functools.partial(shards, ring, mesh.shape["dp"]),
        mesh=mesh,
        in_specs=(
            P("dp", "mp", None, None),
            P(),
            P(None, None, None, "mp", None),
            P("dp", None, None, None, "mp"),
        ),
        out_specs=(P("dp", None, None, None, "mp"), P(), P(None, None, None, "mp", None)),
        check_vma=False,
    )
```

time: 853 us -> 65.1 us (0.08); the launches traced: 838 us -> 64.8 us
  waiting for transfers between devices: 343 us -> 0 us
  local copies, waits for them, and re-layouts: 263 us -> 7.28 us
  matrix products: 137 us -> 0 us
  other arithmetic: 66 us -> 0 us
  Pallas kernels: 0 us -> 56.9 us
  starting transfers between devices: 15.2 us -> 0 us
  between operations: 14.4 us -> 0.65 us
    psum x2 -> x0, waiting for transfers between devices: 192 us -> none  [the longest x1 147 us: shards(): total_a = lax.psum(local_a, ('mp', 'dp'))]
    transpose x2 -> x0, matrix products: 98.3 us -> none  [kernel_grad(): return jnp.transpose(result, (1, 2, 3, 0, 4))]
    all_gather x1 -> x0, waiting for transfers between devices: 97.7 us -> none  [shards(): upstream = lax.all_gather(cotangent, 'mp', axis=4, tiled=True)]
    unnamed x32 -> x11, local copies, waits for them, and re-layouts: 66.3 us -> 7.28 us
    concatenate x1 -> x0, other arithmetic: 58.2 us -> none  [shards(): padded_x = pad_sides(jnp.concatenate([below, field], axis=1))]
    pallas_call x0 -> x1, Pallas kernels: none -> 56.9 us  [shards(): pl.pallas_call(functools.partial(body, ring, scale_a, scale_b), out_shape...]
    conv_general_dilated x9 -> x0, local copies, waits for them, and re-layouts: 52.2 us -> none  [the longest x6 38.1 us: forward_conv(): lax.conv_general_dilated(padded, kernel, (2, 2, 2), 'VALID', dimension_nu...]
    unnamed x5 -> x0, waiting for transfers between devices: 51.4 us -> none
  transfers between devices with their start and end apart: 7 -> 0, of which waited for: 5 -> 0; matrix products, arithmetic and copies ran while one was open for 32% -> 0% of each run, Pallas kernels for 0% -> 0%
where the time goes in v1:
time: 65.1 us; the launch traced here: 64.8 us
  Pallas kernels  56.9 us (87%)
  local copies, waits for them, and re-layouts  7.28 us (11%)
    pallas_call x1, Pallas kernels, shards(): pl.pallas_call(functools.partial(body, ring, scale_a, scale_b), out_shape...  56.9 us
    unnamed x11, local copies, waits for them, and re-layouts  7.28 us

profile of v1, /device:TPU:1, one launch (start us, length us, event | category | flops | bytes accessed | tf_op | source)
XLA Modules:
  0.0 64.8 jit_solution(13175763059206406924)
XLA Ops:
  0.6 0.0 copy-start
  0.6 1.6 %copy-done = bf16[1,8,64,2048]{3,2,1,0:T(8,128)(2,1)S(1)} copy-done((bf16[1,8,64,2048]{3,2,1,0:T(8,128)(2,1)S(1)}, bf16[1,8,64,2048]{3,2,1,0:T(8,128)(2,1)}, u32[]{:S(2)}) %copy-start) | copy-done | bytes 2097176
  2.2 0.0 copy-start.1
  2.2 1.2 %copy-done.1 = bf16[1,16,16,16,16]{4,3,2,1,0:T(8,128)(2,1)S(1)} copy-done((bf16[1,16,16,16,16]{4,3,2,1,0:T(8,128)(2,1)S(1)}, bf16[1,16,16,16,16]{4,3,2,1,0:T(8,128)(2,1)}, u32[]{:S(2)}) %copy-start.1) | copy-done | bytes 131096
  3.4 0.0 copy-start.2
  3.5 0.9 %copy-done.2 = bf16[3,3,3,32,64]{4,3,2,1,0:T(8,128)(2,1)S(1)} copy-done((bf16[3,3,3,32,64]{4,3,2,1,0:T(8,128)(2,1)S(1)}, bf16[3,3,3,32,64]{4,3,2,1,0:T(8,128)(2,1)}, u32[]{:S(2)}) %copy-start.2) | copy-done | bytes 110616
  4.4 0.0 copy-start.3
  4.4 0.8 %copy-done.3 = bf16[3,3,3,8,128]{4,3,2,1,0:T(8,128)(2,1)S(1)} copy-done((bf16[3,3,3,8,128]{4,3,2,1,0:T(8,128)(2,1)S(1)}, bf16[3,3,3,8,128]{4,3,2,1,0:T(8,128)(2,1)}, u32[]{:S(2)}) %copy-start.3) | copy-done | bytes 55320
  5.2 56.9 %shard_map.67 = (bf16[16,4096]{1,0:T(8,128)(2,1)S(1)}, f32[27,32,64]{2,1,0:T(8,128)S(1)}, f32[216,128]{1,0:T(8,128)S(1)}) custom-call(bf16[8,64,2048]{2,1,0:T(8,128)(2,1)S(1)} %bitcast.11, bf16[9,96,64]{2,1,0:T(8,128)(2,1)S(1)} %bitcast.13, bf16[216,128]{1,0:T(8,128)(2,1)S(1)} %bitcast.14, bf16[4096,16]{1,0:T(8,128)(2,1)S(1)} %bitcast.12), custom_call_target="tpu_custom_call" | custom-call | flops 1600000000 | bytes 4000000 | tf_op jit(solution)/shard_map/pallas_call | solution.py:498
  62.1 1.3 %copy.8 = bf16[4096,16]{1,0:T(8,128)(2,1)} copy(bf16[4096,16]{0,1:T(8,128)(2,1)S(1)} %bitcast.9) | data formatting | bytes 262144
  63.4 0.8 %copy.11 = f32[3,3,3,32,64]{4,3,2,1,0:T(8,128)} copy(f32[3,3,3,32,64]{4,3,2,1,0:T(8,128)S(1)} %bitcast.8) | data formatting | bytes 442368
  64.2 0.6 copy.12
Async XLA Ops:
  0.6 1.6 %copy-start = (bf16[1,8,64,2048]{3,2,1,0:T(8,128)(2,1)S(1)}, bf16[1,8,64,2048]{3,2,1,0:T(8,128)(2,1)}, u32[]{:S(2)}) copy-start(bf16[1,8,64,2048]{3,2,1,0:T(8,128)(2,1)} %param.4) | copy-start | bytes 6291460
  2.2 1.2 %copy-start.1 = (bf16[1,16,16,16,16]{4,3,2,1,0:T(8,128)(2,1)S(1)}, bf16[1,16,16,16,16]{4,3,2,1,0:T(8,128)(2,1)}, u32[]{:S(2)}) copy-start(bf16[1,16,16,16,16]{4,3,2,1,0:T(8,128)(2,1)} %param.7) | copy-start | bytes 393220
  3.4 0.9 %copy-start.2 = (bf16[3,3,3,32,64]{4,3,2,1,0:T(8,128)(2,1)S(1)}, bf16[3,3,3,32,64]{4,3,2,1,0:T(8,128)(2,1)}, u32[]{:S(2)}) copy-start(bf16[3,3,3,32,64]{4,3,2,1,0:T(8,128)(2,1)} %param.5) | copy-start | bytes 331780
  4.4 0.8 %copy-start.3 = (bf16[3,3,3,8,128]{4,3,2,1,0:T(8,128)(2,1)S(1)}, bf16[3,3,3,8,128]{4,3,2,1,0:T(8,128)(2,1)}, u32[]{:S(2)}) copy-start(bf16[3,3,3,8,128]{4,3,2,1,0:T(8,128)(2,1)} %param.6) | copy-start | bytes 165892

commit v2 on v1

--- a/solution.py
+++ b/solution.py
@@ -51,13 +51,18 @@
     scale_a,
     scale_b,
     x,
+    ka_hbm,
+    kb_hbm,
+    cot_hbm,
+    feat,
+    ga,
+    gb,
+    feat_v,
+    ga_v,
+    xv,
     ka,
     kb,
     cot,
-    feat,
-    ga,
-    gb,
-    xv,
     xs,
     xt,
     wa,
@@ -66,6 +71,7 @@
     ht,
     ct_loc,
     ct_all,
+    kb_half,
     kb_all,
     kb_f,
     wb,
@@ -80,22 +86,25 @@
     gb_1,
     gb_2s,
     gb_2,
-    gb_3,
     ga_f,
     ga_s,
     ga_1,
     ga_2s,
     ga_2,
-    ga_3,
+    ga_3s,
+    ga_3r,
+    gb_3r,
     x_sem,
+    in_sem,
+    out_sem,
     xh_send,
     xh_recv,
-    hh_send,
-    hh_recv,
     ct_send,
     ct_recv,
     kb_send,
     kb_recv,
+    kc_send,
+    kc_recv,
     ft_send,
     ft_recv,
     b1_send,
@@ -143,9 +152,20 @@
     def plane_copy(plane):
         return pltpu.make_async_copy(x.at[plane], xv.at[plane + 1], x_sem.at[plane])
 
+    in_cot = pltpu.make_async_copy(cot_hbm, cot, in_sem.at[0])
+    in_kb = pltpu.make_async_copy(kb_hbm, kb, in_sem.at[1])
+    in_ka = pltpu.make_async_copy(ka_hbm, ka, in_sem.at[2])
+    in_cot.start()
+    in_kb.start()
+    in_ka.start()
+
     @pl.loop(0, 8)
     def _(step):
         plane_copy(7 - step).start()
+
+    in_kb.wait()
+    in_ka.wait()
+    in_cot.wait()
 
     eye = (
         lax.broadcasted_iota(jnp.int32, (16, 16), 0) == lax.broadcasted_iota(jnp.int32, (16, 16), 1)
@@ -157,22 +177,27 @@
         ct_loc[:, pl.ds(pl.multiple_of(pair * 512, 512), 512)] = dot_nt(eye, rows).astype(BF)
 
     ct_loc[:, 4096:4352] = jnp.zeros((16, 256), BF)
-    kb_all[mp] = jnp.concatenate([kb[...].astype(F32), jnp.zeros((8, 128), F32)], axis=0).astype(BF)
+    share = jnp.concatenate([kb[...].astype(F32), jnp.zeros((8, 128), F32)], axis=0).astype(BF)
+    kb_half[0] = share[:ROWS_B]
+    kb_half[1] = share[ROWS_B:]
+    kb_all[core, mp] = kb_half[core]
 
     pl.semaphore_wait(barrier, GROUP - 1 + ring - 1)
 
     def x_halo():
         return remote(x.at[7], xv.at[0], xh_send, xh_recv, in_slabs(mp + 1))
-
-    def h_halo():
-        return remote(hs.at[4, pl.ds(1, 2)], hs.at[0, pl.ds(1, 2)], hh_send, hh_recv, in_slabs(mp + 1))
 
     def ct_copy(peer, slot):
         src = ct_loc.at[:, pl.ds(pl.multiple_of(peer * 512, 512), 768)]
         return remote(src, ct_all.at[slot], ct_send.at[peer], ct_recv.at[slot], in_slabs(peer))
 
     def kb_copy(peer, slot):
-        return remote(kb_all.at[mp], kb_all.at[slot], kb_send.at[peer], kb_recv.at[slot], in_slabs(peer))
+        return remote(
+            kb_all.at[core, mp], kb_all.at[core, slot], kb_send.at[peer], kb_recv.at[slot], in_slabs(peer)
+        )
+
+    def kc_copy(half):
+        return remote(kb_all.at[half], kb_all.at[half], kc_send, kc_recv, in_group(mp * CORES + 1 - core))
 
     def ft_copy(peer, slot):
         return remote(ft.at[peer], fr.at[slot], ft_send.at[peer], ft_recv.at[slot], in_slabs(peer))
@@ -184,7 +209,7 @@
         return remote(gb_2s, gb_2.at[slot], b2_send.at[peer], b2_recv.at[slot], in_ring(peer))
 
     def b3_copy(slot):
-        return remote(gb_3.at[core], gb_3.at[slot], b3_send, b3_recv, in_group(mp * CORES + 1 - core))
+        return remote(gb_3r.at[core], gb_3r.at[slot], b3_send, b3_recv, in_group(mp * CORES + 1 - core))
 
     def a1_copy(peer, slot):
         return remote(ga_s.at[peer], ga_1.at[slot], a1_send.at[peer], a1_recv.at[slot], in_group(peer))
@@ -193,14 +218,14 @@
         return remote(ga_2s, ga_2.at[slot], a2_send.at[peer], a2_recv.at[slot], in_ring(peer))
 
     def a3_copy(peer, slot):
-        return remote(ga_3.at[me], ga_3.at[slot], a3_send.at[peer], a3_recv.at[slot], in_group(peer))
+        return remote(ga_3s, ga_3r.at[slot], a3_send.at[peer], a3_recv.at[slot], in_group(peer))
 
     @pl.when(mp < SLABS - 1)
     def _():
         x_halo().start()
 
+    others(SLABS, mp, lambda i: ct_copy(i, mp).start())
     others(SLABS, mp, lambda i: kb_copy(i, mp).start())
-    others(SLABS, mp, lambda i: ct_copy(i, mp).start())
     ct_all[mp] = ct_loc[:, pl.ds(pl.multiple_of(mp * 512, 512), 768)]
 
     @pl.loop(0, 9)
@@ -224,28 +249,7 @@
             for q in range(16):
                 xs[index, s, q * 16 : q * 16 + 16, :] = rows[s * 16 : s * 16 + 16, q * 128 : q * 128 + 128]
 
-    plane_copy(7).wait()
-    prepare(8)
-
-    @pl.loop(0, 4)
-    def _(step):
-        depth = 3 - step
-        plane_copy(2 * depth).wait()
-        prepare(2 * depth + 1)
-
-        @pl.when(depth > 0)
-        def _():
-            plane_copy(2 * depth - 1).wait()
-
-        @pl.when(jnp.logical_and(depth == 0, mp > 0))
-        def _():
-            x_halo().wait_recv()
-
-        @pl.when(jnp.logical_and(depth == 0, mp == 0))
-        def _():
-            xv[0] = jnp.zeros((64, 2048), BF)
-
-        prepare(2 * depth)
+    def convolve(depth):
         weights = wa[...].reshape(9 * 128, 256)
         for rh in range(2):
             parts = [xs[2 * depth + a, 2 * rh + b] for a in range(3) for b in range(3)]
@@ -253,34 +257,40 @@
             pre = both[:, :128] + later(both[:, 128:])
             pf[depth, rh] = pre
             hidden = jnp.where(pre > 0, pre, 0.3 * pre).astype(BF)
-            hs[depth + 1, rh + 1] = hidden
+            hs[depth, rh + 1] = hidden
             if rh == 1:
-                hs[depth + 1, 0] = row_below(hidden)
-
-        @pl.when(jnp.logical_and(depth == 3, mp < SLABS - 1))
-        def _():
-            h_halo().start()
-
-    @pl.loop(0, 9)
-    def _(index):
+                hs[depth, 0] = row_below(hidden)
+
+    plane_copy(7).wait()
+    prepare(8)
+
+    @pl.loop(0, 3)
+    def _(step):
+        depth = 3 - step
+        plane_copy(2 * depth).wait()
+        prepare(2 * depth + 1)
+        plane_copy(2 * depth - 1).wait()
+        prepare(2 * depth)
+        convolve(depth)
+
+    plane_copy(0).wait()
+    prepare(1)
+
+    def turn_x(index):
         for s in range(5):
             xt[index, s] = xs[index, s].T
 
-    others(SLABS, mp, lambda i: kb_copy(i, i).wait_recv())
-
-    @pl.loop(0, 8)
-    def _(e):
-        kb_f[e] = kb_all[e].astype(F32)
-
-    @pl.loop(0, 9)
-    def _(ab):
-        k0, k1, k2 = [
-            kb_f[:, pl.ds(pl.multiple_of(ab * 24 + c * 8, 8), 8), :].reshape(64, 128) for c in range(3)
-        ]
-        this = jnp.concatenate([k1, k2], axis=0)
-        last = jnp.concatenate([jnp.zeros((64, 128), F32), k0], axis=0)
-        wb[ab] = jnp.concatenate([this, last], axis=1).astype(BF)
-        vb[ab] = jnp.concatenate([this.T, last.T], axis=1).astype(BF)
+    def turn_h(index):
+        for b in range(3):
+            ht[index, b] = hs[index, b].T
+
+    @pl.loop(1, 9)
+    def _(index):
+        turn_x(index)
+
+    @pl.loop(1, 4)
+    def _(index):
+        turn_h(index)
 
     others(SLABS, mp, lambda i: ct_copy(i, i).wait_recv())
     order_row = lax.broadcasted_iota(jnp.int32, (512, 256), 0)
@@ -294,48 +304,39 @@
         both = dot_nt(order, lanes).astype(BF)
         cs[p, 0] = both[:256]
         cs[p, 1] = both[256:]
-        if p < 2:
-            cc[p] = jnp.concatenate([both[:256], earlier(both[:256])], axis=1)
+        cc[p] = jnp.concatenate([both[:256], earlier(both[:256])], axis=1)
 
     @pl.when(mp > 0)
     def _():
-        h_halo().wait_recv()
+        x_halo().wait_recv()
 
     @pl.when(mp == 0)
     def _():
-        hs[0] = jnp.zeros((3, 256, 128), BF)
-
-    hs[0, 0] = row_below(hs[0, 2])
-
-    @pl.loop(0, 5)
-    def _(index):
-        for b in range(3):
-            ht[index, b] = hs[index, b].T
-
-    @pl.loop(0, 2)
-    def _(depth):
-        parts = [hs[2 * depth + a, b] for a in range(3) for b in range(3)]
-        both = dot(jnp.concatenate(parts, axis=1), wb[...].reshape(9 * 128, 256))
-        out = (both[:, :128] + later(both[:, 128:])).astype(BF)
-        turned = dot_tn(out, order[:256]).astype(BF)
-        ft[:, :, pl.ds(pl.multiple_of(depth * 256, 256), 256)] = turned.reshape(8, 16, 256)
-
-    others(SLABS, mp, lambda i: ft_copy(i, mp).start())
-    fr[mp] = ft[mp]
-
-    @pl.loop(0, 3)
-    def _(a):
+        xv[0] = jnp.zeros((64, 2048), BF)
+
+    prepare(0)
+    convolve(0)
+    turn_h(0)
+
+    others(SLABS, mp, lambda i: kb_copy(i, i).wait_recv())
+    kc_copy(core).start()
+
+    def grad_b_rows(a, planes, cots):
         lhs = jnp.concatenate(
-            [jnp.concatenate([ht[2 * p + a, b] for b in range(3)], axis=0) for p in range(2)], axis=1
+            [jnp.concatenate([ht[plane, b] for b in range(3)], axis=0) for plane in planes], axis=1
         )
-        acc = dot(lhs, cc[...].reshape(512, 256))
+        rhs = jnp.concatenate([cc[p] for p in cots], axis=0)
+        acc = dot(lhs, rhs)
         for b in range(3):
             block = acc[b * 128 : b * 128 + 128]
             pieces = (block[64:, 128:], block[:64, :128], block[64:, :128])
             for c in range(3):
-                start = pl.multiple_of(a * 72 + b * 24 + c * 8, 8)
-                gb_f[:, pl.ds(start, 8), :] = pieces[c].reshape(8, 8, 128)
-
+                start = a * 72 + b * 24 + c * 8
+                gb_f[:, start : start + 8, :] = pieces[c].reshape(8, 8, 128)
+
+    grad_b_rows(0, (1, 3), (1, 2))
+    grad_b_rows(1, (0, 2), (0, 1))
+    grad_b_rows(2, (1, 3), (0, 1))
     gb_f[:, 216:224, :] = jnp.zeros((8, 8, 128), F32)
 
     @pl.loop(0, 8)
@@ -345,6 +346,24 @@
 
     others(GROUP, me, lambda i: b1_copy(i, me).start())
     gb_1[me] = gb_s[me]
+    turn_x(0)
+
+    kc_copy(1 - core).wait_recv()
+
+    @pl.loop(0, 8)
+    def _(e):
+        kb_f[e, 0:ROWS_B] = kb_all[0, e].astype(F32)
+        kb_f[e, ROWS_B : 2 * ROWS_B] = kb_all[1, e].astype(F32)
+
+    @pl.loop(0, 9)
+    def _(ab):
+        k0, k1, k2 = [
+            kb_f[:, pl.ds(pl.multiple_of(ab * 24 + c * 8, 8), 8), :].reshape(64, 128) for c in range(3)
+        ]
+        this = jnp.concatenate([k1, k2], axis=0)
+        last = jnp.concatenate([jnp.zeros((64, 128), F32), k0], axis=0)
+        wb[ab] = jnp.concatenate([this, last], axis=1).astype(BF)
+        vb[ab] = jnp.concatenate([this.T, last.T], axis=1).astype(BF)
 
     @pl.loop(0, 2)
     def _(depth):
@@ -359,11 +378,6 @@
                 slope = jnp.where(pf[2 * depth + rd, rh] > 0, 1.0, 0.3)
                 delta = back * slope
                 dd[2 * depth + rd, rh] = jnp.concatenate([delta, earlier(delta)], axis=1).astype(BF)
-
-    others(GROUP, me, lambda i: b1_copy(i, i).wait_recv())
-    gb_2s[...] = jnp.sum(gb_1[...].astype(F32), axis=0)
-    others(ring, rank, lambda i: b2_copy(i, rank).start())
-    gb_2[rank] = gb_2s[...]
 
     lane = lax.broadcasted_iota(jnp.int32, (16, 128), 1)
 
@@ -392,46 +406,103 @@
     others(GROUP, me, lambda i: a1_copy(i, me).start())
     ga_1[me] = ga_s[me]
 
-    others(ring, rank, lambda i: b2_copy(i, i).wait_recv())
-    gb_3[core] = jnp.sum(gb_2[...], axis=0) * scale_b
-    b3_copy(core).start()
+    def features_of(plane, terms):
+        lhs = [hs[p, b] for p, _ in terms for b in range(3)]
+        rhs = [wb[a * 3 + b] for _, a in terms for b in range(3)]
+        both = dot(jnp.concatenate(lhs, axis=1), jnp.concatenate(rhs, axis=0))
+        out = (both[:, :128] + later(both[:, 128:])).astype(BF)
+        turned = dot_tn(out, order[:256]).astype(BF)
+        ft[:, :, plane * 256 : plane * 256 + 256] = turned.reshape(8, 16, 256)
+
+    features_of(0, [(0, 1), (1, 2)])
+    features_of(1, [(1, 0), (2, 1), (3, 2)])
+    features_of(2, [(3, 0)])
+    others(SLABS, mp, lambda i: ft_copy(i, mp).start())
+    fr[mp] = ft[mp]
+
+    others(GROUP, me, lambda i: b1_copy(i, i).wait_recv())
+    gb_2s[...] = jnp.sum(gb_1[...].astype(F32), axis=0).astype(BF)
+    others(ring, rank, lambda i: b2_copy(i, rank).start())
+    gb_2[rank] = gb_2s[...]
 
     others(GROUP, me, lambda i: a1_copy(i, i).wait_recv())
     ga_2s[...] = jnp.sum(ga_1[...].astype(F32), axis=0)
     others(ring, rank, lambda i: a2_copy(i, rank).start())
     ga_2[rank] = ga_2s[...]
 
+    others(ring, rank, lambda i: b2_copy(i, i).wait_recv())
+    gb_3r[core] = jnp.sum(gb_2[...].astype(F32), axis=0) * scale_b
+    b3_copy(core).start()
+
+    others(ring, rank, lambda i: a2_copy(i, i).wait_recv())
+    ga_3s[...] = (jnp.sum(ga_2[...], axis=0) * scale_a).astype(BF)
+    others(GROUP, me, lambda i: a3_copy(i, me).start())
+    ga_3r[me] = ga_3s[...]
+
     others(SLABS, mp, lambda i: ft_copy(i, i).wait_recv())
     for e in range(SLABS):
-        feat[:, e * 512 : e * 512 + 512] = fr[e]
-
-    b3_copy(1 - core).wait_recv()
-    gb[0:ROWS_B, :] = gb_3[0]
-    gb[ROWS_B:216, :] = gb_3[1, : 216 - ROWS_B, :]
-
-    others(ring, rank, lambda i: a2_copy(i, i).wait_recv())
-    ga_3[me] = jnp.sum(ga_2[...], axis=0) * scale_a
-    others(GROUP, me, lambda i: a3_copy(i, me).start())
+        first = fr[e, :, 0:256].astype(F32)
+        if e > 0:
+            first = first + fr[e - 1, :, 512:768].astype(F32)
+        planes = jnp.concatenate([first.astype(BF), fr[e, :, 256:512]], axis=1)
+        feat_v[e * 512 : e * 512 + 512, :] = dot_tn(planes, eye).astype(BF)
+
+    out_feat = pltpu.make_async_copy(feat_v, feat, out_sem.at[0])
+    out_feat.start()
 
     @pl.when(mp < SLABS - 1)
     def _():
         x_halo().wait_send()
-        h_halo().wait_send()
 
     others(SLABS, mp, lambda i: kb_copy(i, mp).wait_send())
+    kc_copy(core).wait_send()
     others(SLABS, mp, lambda i: ct_copy(i, mp).wait_send())
     others(SLABS, mp, lambda i: ft_copy(i, mp).wait_send())
     others(GROUP, me, lambda i: b1_copy(i, me).wait_send())
     others(ring, rank, lambda i: b2_copy(i, rank).wait_send())
-    b3_copy(core).wait_send()
     others(GROUP, me, lambda i: a1_copy(i, me).wait_send())
     others(ring, rank, lambda i: a2_copy(i, rank).wait_send())
 
+    b3_copy(1 - core).wait_recv()
+    out_gb = pltpu.make_async_copy(gb_3r, gb, out_sem.at[1])
+    out_gb.start()
+    b3_copy(core).wait_send()
     others(GROUP, me, lambda i: a3_copy(i, i).wait_recv())
-    whole = ga_3[...].reshape(GROUP * ROWS_A, 128)[:432].reshape(27, 16, 128)
-    ga[:, 0:16, :] = whole[:, :, :64]
-    ga[:, 16:32, :] = whole[:, :, 64:]
+    whole = ga_3r[...].astype(F32).reshape(GROUP * ROWS_A, 128)[:432].reshape(27, 16, 128)
+    ga_v[:, 0:16, :] = whole[:, :, :64]
+    ga_v[:, 16:32, :] = whole[:, :, 64:]
+    out_ga = pltpu.make_async_copy(ga_v, ga, out_sem.at[2])
+    out_ga.start()
     others(GROUP, me, lambda i: a3_copy(i, me).wait_send())
+    out_feat.wait()
+    out_gb.wait()
+    out_ga.wait()
+
+
+def finish(feat_in, ga_in, gb_in, feat, ga, gb, feat_v, ga_v, gb_v, in_sem, out_sem):
+    rest = 216 - ROWS_B
+    inward = [
+        pltpu.make_async_copy(feat_in, feat_v, in_sem.at[0]),
+        pltpu.make_async_copy(ga_in, ga_v, in_sem.at[1]),
+        pltpu.make_async_copy(gb_in.at[0], gb_v.at[pl.ds(0, ROWS_B)], in_sem.at[2]),
+        pltpu.make_async_copy(gb_in.at[1, pl.ds(0, rest)], gb_v.at[pl.ds(ROWS_B, rest)], in_sem.at[3]),
+    ]
+    outward = [
+        pltpu.make_async_copy(feat_v, feat, out_sem.at[0]),
+        pltpu.make_async_copy(ga_v, ga, out_sem.at[1]),
+        pltpu.make_async_copy(gb_v, gb, out_sem.at[2]),
+    ]
+    for copy in inward:
+        copy.start()
+    inward[0].wait()
+    outward[0].start()
+    inward[1].wait()
+    outward[1].start()
+    inward[2].wait()
+    inward[3].wait()
+    outward[2].start()
+    for copy in outward:
+        copy.wait()
 
 
 def shards(ring, samples, volume, kernel_a, kernel_b, cotangent):
@@ -440,45 +511,54 @@
     vmem = pltpu.VMEM
     dma = pltpu.SemaphoreType.DMA
     scratch = [
+        vmem((4096, 16), BF),
+        vmem((27, 32, 64), F32),
         vmem((9, 64, 2048), BF),
+        vmem((9, 96, 64), BF),
+        vmem((216, 128), BF),
+        vmem((4096, 16), BF),
         vmem((9, 5, 256, 128), BF),
         vmem((9, 5, 128, 256), BF),
         vmem((9, 128, 256), BF),
         vmem((4, 2, 256, 128), F32),
-        vmem((5, 3, 256, 128), BF),
-        vmem((5, 3, 128, 256), BF),
+        vmem((4, 3, 256, 128), BF),
+        vmem((4, 3, 128, 256), BF),
         vmem((16, 4352), BF),
         vmem((8, 16, 768), BF),
-        vmem((8, 224, 128), BF),
+        vmem((CORES, ROWS_B, 128), BF),
+        vmem((CORES, 8, ROWS_B, 128), BF),
         vmem((8, 224, 128), F32),
         vmem((9, 128, 256), BF),
         vmem((9, 128, 256), BF),
         vmem((3, 2, 256, 128), BF),
-        vmem((2, 256, 256), BF),
-        vmem((8, 16, 512), BF),
-        vmem((8, 16, 512), BF),
+        vmem((3, 256, 256), BF),
+        vmem((8, 16, 768), BF),
+        vmem((8, 16, 768), BF),
         vmem((4, 2, 256, 256), BF),
         vmem((8, 224, 128), F32),
         vmem((GROUP, ROWS_B, 128), BF),
         vmem((GROUP, ROWS_B, 128), BF),
-        vmem((ROWS_B, 128), F32),
-        vmem((ring, ROWS_B, 128), F32),
-        vmem((CORES, ROWS_B, 128), F32),
+        vmem((ROWS_B, 128), BF),
+        vmem((ring, ROWS_B, 128), BF),
         vmem((512, 128), F32),
         vmem((GROUP, ROWS_A, 128), BF),
         vmem((GROUP, ROWS_A, 128), BF),
         vmem((ROWS_A, 128), F32),
         vmem((ring, ROWS_A, 128), F32),
-        vmem((GROUP, ROWS_A, 128), F32),
+        vmem((ROWS_A, 128), BF),
+        vmem((GROUP, ROWS_A, 128), BF),
+        vmem((CORES, ROWS_B, 128), F32),
         dma((8,)),
-        dma,
-        dma,
+        dma((3,)),
+        dma((3,)),
         dma,
         dma,
         dma((8,)),
         dma((8,)),
         dma((8,)),
         dma((8,)),
+        dma,
+        dma,
         dma((8,)),
         dma((8,)),
         dma((GROUP,)),
@@ -494,19 +574,19 @@
         dma((GROUP,)),
         dma((GROUP,)),
     ]
-    in_vmem = pl.BlockSpec(memory_space=pltpu.VMEM)
-    feat, ga, gb = pl.pallas_call(
+    in_hbm = pl.BlockSpec(memory_space=pltpu.HBM)
+    parts = pl.pallas_call(
         functools.partial(body, ring, scale_a, scale_b),
         out_shape=(
-            jax.ShapeDtypeStruct((16, 4096), BF),
+            jax.ShapeDtypeStruct((4096, 16), BF),
             jax.ShapeDtypeStruct((27, 32, 64), F32),
-            jax.ShapeDtypeStruct((216, 128), F32),
+            jax.ShapeDtypeStruct((CORES, ROWS_B, 128), F32),
         ),
-        in_specs=[pl.BlockSpec(memory_space=pl.ANY), in_vmem, in_vmem, in_vmem],
-        out_specs=(in_vmem, in_vmem, in_vmem),
+        in_specs=[in_hbm] * 4,
+        out_specs=(in_hbm, in_hbm, in_hbm),
         scratch_shapes=scratch,
         compiler_params=pltpu.CompilerParams(
-            collective_id=0, has_side_effects=True, vmem_limit_bytes=48 * 1024 * 1024
+            collective_id=0, has_side_effects=True, vmem_limit_bytes=60 * 1024 * 1024
         ),
         cost_estimate=pl.CostEstimate(flops=1600000000, bytes_accessed=4000000, transcendentals=0),
     )(
@@ -515,8 +595,29 @@
         kernel_b.reshape(216, 128),
         cotangent.reshape(4096, 16),
     )
-    features = feat.T.reshape(1, 16, 16, 16, 16)
-    return (features, ga.reshape(3, 3, 3, 32, 64), gb.reshape(3, 3, 3, 8, 128))
+    feat, ga, gb = pl.pallas_call(
+        finish,
+        out_shape=(
+            jax.ShapeDtypeStruct((4096, 16), BF),
+            jax.ShapeDtypeStruct((27, 32, 64), F32),
+            jax.ShapeDtypeStruct((216, 128), F32),
+        ),
+        in_specs=[in_hbm] * 3,
+        out_specs=(in_hbm, in_hbm, in_hbm),
+        scratch_shapes=[
+            vmem((4096, 16), BF),
+            vmem((27, 32, 64), F32),
+            vmem((216, 128), F32),
+            dma((4,)),
+            dma((3,)),
+        ],
+        compiler_params=pltpu.CompilerParams(vmem_limit_bytes=60 * 1024 * 1024),
+    )(*parts)
+    return (
+        feat.reshape(1, 16, 16, 16, 16),
+        ga.reshape(3, 3, 3, 32, 64),
+        gb.reshape(3, 3, 3, 8, 128),
+    )
 
 
 def solution(mesh):

time: 65.1 us -> 47.3 us (0.73)
  Pallas kernels: 56.9 us -> 46.5 us
  local copies, waits for them, and re-layouts: 7.28 us -> 0 us
    pallas_call x1, Pallas kernels: 56.9 us -> 44.1 us  [shards(): pl.pallas_call(functools.partial(body, ring, scale_a, scale_b), out_shape...]
    unnamed x11 -> x0, local copies, waits for them, and re-layouts: 7.28 us -> none
    pallas_call x0 -> x1, Pallas kernels: none -> 2.42 us  [shards(): pl.pallas_call(finish, out_shape=(jax.ShapeDtypeStruct((4096, 16), BF), j...]
where the time goes in v2:
time: 47.3 us; the launch traced here: 47.1 us
  Pallas kernels  46.5 us (98%)
  between operations  0.64 us (1%)
    pallas_call x1, Pallas kernels, shards(): pl.pallas_call(functools.partial(body, ring, scale_a, scale_b), out_shape...  44.1 us
    pallas_call x1, Pallas kernels, shards(): pl.pallas_call(finish, out_shape=(jax.ShapeDtypeStruct((4096, 16), BF), j...  2.42 us

profile of v2, /device:TPU:1, one launch (start us, length us, event | category | flops | bytes accessed | tf_op | source)
XLA Modules:
  0.0 47.1 jit_solution(9432652241355425301)
XLA Ops:
  0.6 44.1 %shard_map.67 = (bf16[4096,16]{1,0:T(8,128)(2,1)}, f32[27,32,64]{2,1,0:T(8,128)}, f32[2,112,128]{2,1,0:T(8,128)}) custom-call(bf16[8,64,2048]{2,1,0:T(8,128)(2,1)} %bitcast.7, bf16[9,96,64]{2,1,0:T(8,128)(2,1)} %bitcast.11, bf16[216,128]{1,0:T(8,128)(2,1)} %bitcast.13, bf16[4096,16]{1,0:T(8,128)(2,1)} %bitcast.8), custom_call_target="tpu_custom_call" | custom-call | flops 1600000000 | bytes 4000000 | tf_op jit(solution)/shard_map/pallas_call | solution.py:578
  44.7 2.4 %shard_map.68 = (bf16[4096,16]{1,0:T(8,128)(2,1)}, f32[27,32,64]{2,1,0:T(8,128)}, f32[216,128]{1,0:T(8,128)}) custom-call(bf16[4096,16]{1,0:T(8,128)(2,1)} %get-tuple-element.9.feat_in, f32[27,32,64]{2,1,0:T(8,128)} %get-tuple-element.10.ga_in, f32[2,112,128]{2,1,0:T(8,128)} %get-tuple-element.11.gb_in), custom_call_target="tpu_custom_call" | custom-call | tf_op jit(solution)/shard_map/pallas_call | solution.py:598

commit v3 on v2

v3 whole, which is shorter than its diff:
```python
import functools
import math

import jax
import jax.numpy as jnp
from jax import lax
from jax.experimental import pallas as pl
from jax.experimental.pallas import tpu as pltpu
from jax.sharding import PartitionSpec as P

BF = jnp.bfloat16
F32 = jnp.float32
MESH = pl.DeviceIdType.MESH
SLABS = 8
CORES = 2
GROUP = SLABS * CORES
HALF = 112
ROWS_E = 80
ROWS_L = 48
ROWS_A = 32


def dot(lhs, rhs):
    return jnp.dot(lhs, rhs, preferred_element_type=F32)


def dot_nt(lhs, rhs):
    return lax.dot_general(lhs, rhs, (((1,), (1,)), ((), ())), preferred_element_type=F32)


def dot_tn(lhs, rhs):
    return lax.dot_general(lhs, rhs, (((0,), (0,)), ((), ())), preferred_element_type=F32)


def later(tiles):
    zero = jnp.zeros((16, tiles.shape[1]), tiles.dtype)
    return jnp.concatenate([zero, tiles[:-16]], axis=0)


def earlier(tiles):
    zero = jnp.zeros((16, tiles.shape[1]), tiles.dtype)
    return jnp.concatenate([tiles[16:], zero], axis=0)


def row_below(tiles):
    rolled = pltpu.roll(tiles.astype(F32), 1, 0)
    row = lax.broadcasted_iota(jnp.int32, tiles.shape, 0)
    return jnp.where(lax.rem(row, 16) == 0, 0.0, rolled).astype(BF)


def body(
    ring,
    scale_a,
    scale_b,
    x,
    ka_hbm,
    kb_hbm,
    cot_hbm,
    feat,
    ga,
    gbe,
    gbl,
    xv,
    ka,
    kb,
    cot,
    xs,
    xt,
    wa,
    pf,
    hs,
    ht,
    ct_loc,
    ct_all,
    kb_half,
    kb_all,
    kb_f,
    wb,
    vb,
    cs,
    cc,
    ft_up,
    fr_up,
    ft_low,
    fr_low,
    dd,
    bk,
    acc_a,
    ge_f,
    ge_s,
    ge_0,
    ge_h,
    ge_1,
    ge_2s,
    ge_2,
    ge_3,
    gl_f,
    gl_s,
    gl_0,
    gl_h,
    gl_1,
    gl_2s,
    gl_2,
    gl_3,
    ga_f,
    ga_s,
    ga_1,
    ga_2s,
    ga_2,
    ga_3s,
    ga_3,
    x_sem,
    in_sem,
    xh_send,
    xh_recv,
    ct_send,
    ct_recv,
    kb_send,
    kb_recv,
    kc_send,
    kc_recv,
    fu_send,
    fu_recv,
    fl_send,
    fl_recv,
    e0_send,
    e0_recv,
    e1_send,
    e1_recv,
    e2_send,
    e2_recv,
    e3_send,
    e3_recv,
    l0_send,
    l0_recv,
    l1_send,
    l1_recv,
    l2_send,
    l2_recv,
    l3_send,
    l3_recv,
    a1_send,
    a1_recv,
    a2_send,
    a2_recv,
    a3_send,
    a3_recv,
):
    mp = lax.axis_index("mp")
    dp = lax.axis_index("dp")
    core = lax.rem(dp, CORES)
    rank = lax.div(dp, CORES)
    me = mp * CORES + core

    def in_group(index):
        return {"mp": lax.div(index, CORES), "dp": rank * CORES + lax.rem(index, CORES)}

    def in_slabs(index):
        return {"mp": index, "dp": dp}

    def in_ring(index):
        return {"mp": mp, "dp": index * CORES + core}

    def others(size, mine, act):
        @pl.loop(1, size)
        def _(step):
            act(lax.rem(mine + step, size))

    def remote(src, dst, send, recv, device):
        return pltpu.make_async_remote_copy(
            src_ref=src, dst_ref=dst, send_sem=send, recv_sem=recv, device_id=device, device_id_type=MESH
        )

    barrier = pltpu.get_barrier_semaphore()
    others(GROUP, me, lambda i: pl.semaphore_signal(barrier, inc=1, device_id=in_group(i), device_id_type=MESH))
    others(ring, rank, lambda i: pl.semaphore_signal(barrier, inc=1, device_id=in_ring(i), device_id_type=MESH))

    def plane_copy(plane):
        return pltpu.make_async_copy(x.at[plane], xv.at[plane + 1], x_sem.at[plane])

    in_cot = pltpu.make_async_copy(cot_hbm, cot, in_sem.at[0])
    in_kb = pltpu.make_async_copy(kb_hbm, kb, in_sem.at[1])
    in_ka = pltpu.make_async_copy(ka_hbm, ka, in_sem.at[2])
    in_cot.start()
    in_kb.start()
    in_ka.start()

    @pl.loop(0, 8)
    def _(step):
        plane_copy(7 - step).start()

    in_kb.wait()
    in_ka.wait()
    in_cot.wait()

    eye = (
        lax.broadcasted_iota(jnp.int32, (16, 16), 0) == lax.broadcasted_iota(jnp.int32, (16, 16), 1)
    ).astype(BF)

    @pl.loop(0, 8)
    def _(pair):
        rows = cot[pl.ds(pl.multiple_of(pair * 512, 512), 512), :]
        ct_loc[:, pl.ds(pl.multiple_of(pair * 512, 512), 512)] = dot_nt(eye, rows).astype(BF)

    ct_loc[:, 4096:4352] = jnp.zeros((16, 256), BF)
    share = jnp.concatenate([kb[...].astype(F32), jnp.zeros((8, 128), F32)], axis=0).astype(BF)
    kb_half[0] = share[:HALF]
    kb_half[1] = share[HALF:]
    kb_all[core, mp] = kb_half[core]

    @pl.loop(0, 9)
    def _(ab):
        k0 = ka[ab, 0:32, :]
        k1 = ka[ab, 32:64, :]
        k2 = ka[ab, 64:96, :]
        no = jnp.zeros((32, 64), BF)
        wa[ab, 0:32, :] = jnp.concatenate([k1, no, no, no], axis=1)
        wa[ab, 32:64, :] = jnp.concatenate([k2, k0, no, no], axis=1)
        wa[ab, 64:96, :] = jnp.concatenate([no, k1, no, no], axis=1)
        wa[ab, 96:128, :] = jnp.concatenate([no, k2, k0, no], axis=1)

    pick_row = lax.broadcasted_iota(jnp.int32, (80, 64), 0)
    pick_col = lax.broadcasted_iota(jnp.int32, (80, 64), 1)
    pick = (pick_col == 4 * lax.rem(pick_row, 16) + lax.div(pick_row, 16) - 1).astype(BF)

    def prepare(index):
        rows = dot(pick, xv[index]).astype(BF)
        for s in range(5):
            for q in range(16):
                xs[index, s, q * 16 : q * 16 + 16, :] = rows[s * 16 : s * 16 + 16, q * 128 : q * 128 + 128]

    def convolve(depth):
        weights = wa[...].reshape(9 * 128, 256)
        for rh in range(2):
            parts = [xs[2 * depth + a, 2 * rh + b] for a in range(3) for b in range(3)]
            both = dot(jnp.concatenate(parts, axis=1), weights)
            pre = both[:, :128] + later(both[:, 128:])
            pf[depth, rh] = pre
            hidden = jnp.where(pre > 0, pre, 0.3 * pre).astype(BF)
            hs[depth, rh + 1] = hidden
            if rh == 1:
                hs[depth, 0] = row_below(hidden)

    def both_planes(depth):
        plane_copy(2 * depth).wait()
        prepare(2 * depth + 1)
        plane_copy(2 * depth - 1).wait()
        prepare(2 * depth)
        convolve(depth)

    pl.semaphore_wait(barrier, GROUP - 1 + ring - 1)

    def x_halo():
        return remote(x.at[7], xv.at[0], xh_send, xh_recv, in_slabs(mp + 1))

    def ct_copy(peer, slot):
        src = ct_loc.at[:, pl.ds(pl.multiple_of(peer * 512, 512), 768)]
        return remote(src, ct_all.at[slot], ct_send.at[peer], ct_recv.at[slot], in_slabs(peer))

    def kb_copy(peer, slot):
        return remote(
            kb_all.at[core, mp], kb_all.at[core, slot], kb_send.at[peer], kb_recv.at[slot], in_slabs(peer)
        )

    def kc_copy(half):
        return remote(kb_all.at[half], kb_all.at[half], kc_send, kc_recv, in_group(mp * CORES + 1 - core))

    def fu_copy(peer, slot):
        return remote(ft_up.at[peer], fr_up.at[slot], fu_send.at[peer], fu_recv.at[slot], in_slabs(peer))

    def fl_copy(peer, slot):
        return remote(ft_low.at[peer], fr_low.at[slot], fl_send.at[peer], fl_recv.at[slot], in_slabs(peer))

    def e0_copy():
        return remote(ge_s, ge_0, e0_send, e0_recv, in_group(mp * CORES + 1 - core))

    def e1_copy(peer, slot):
        return remote(ge_h.at[peer], ge_1.at[slot], e1_send.at[peer], e1_recv.at[slot], in_slabs(peer))

    def e2_copy(peer, slot):
        return remote(ge_2s, ge_2.at[slot], e2_send.at[peer], e2_recv.at[slot], in_ring(peer))

    def e3_copy(slot):
        return remote(ge_3.at[core], ge_3.at[slot], e3_send, e3_recv, in_group(mp * CORES + 1 - core))

    def l0_copy():
        return remote(gl_s, gl_0, l0_send, l0_recv, in_group(mp * CORES + 1 - core))

    def l1_copy(peer, slot):
        return remote(gl_h.at[peer], gl_1.at[slot], l1_send.at[peer], l1_recv.at[slot], in_slabs(peer))

    def l2_copy(peer, slot):
        return remote(gl_2s, gl_2.at[slot], l2_send.at[peer], l2_recv.at[slot], in_ring(peer))

    def l3_copy(slot):
        return remote(gl_3.at[core], gl_3.at[slot], l3_send, l3_recv, in_group(mp * CORES + 1 - core))

    def a1_copy(peer, slot):
        return remote(ga_s.at[peer], ga_1.at[slot], a1_send.at[peer], a1_recv.at[slot], in_group(peer))

    def a2_copy(peer, slot):
        return remote(ga_2s, ga_2.at[slot], a2_send.at[peer], a2_recv.at[slot], in_ring(peer))

    def a3_copy(peer, slot):
        return remote(ga_3s, ga_3.at[slot], a3_send.at[peer], a3_recv.at[slot], in_group(peer))

    others(SLABS, mp, lambda i: kb_copy(i, mp).start())
    others(SLABS, mp, lambda i: ct_copy(i, mp).start())

    @pl.when(mp < SLABS - 1)
    def _():
        x_halo().start()

    ct_all[mp] = ct_loc[:, pl.ds(pl.multiple_of(mp * 512, 512), 768)]

    plane_copy(7).wait()
    prepare(8)
    both_planes(3)

    @pl.loop(0, 2)
    def _(step):
        both_planes(2 - step)

    plane_copy(0).wait()
    prepare(1)

    def turn_x(index):
        for s in range(5):
            xt[index, s] = xs[index, s].T

    def turn_h(index):
        for b in range(3):
            ht[index, b] = hs[index, b].T

    @pl.loop(1, 9)
    def _(index):
        turn_x(index)

    @pl.loop(1, 4)
    def _(index):
        turn_h(index)

    others(SLABS, mp, lambda i: kb_copy(i, i).wait_recv())
    kc_copy(core).start()

    others(SLABS, mp, lambda i: ct_copy(i, i).wait_recv())
    order_row = lax.broadcasted_iota(jnp.int32, (512, 256), 0)
    order_col = lax.broadcasted_iota(jnp.int32, (512, 256), 1)
    order_pos = lax.rem(order_row, 256)
    order = (
        order_col == (lax.rem(order_pos, 16) + lax.div(order_row, 256)) * 16 + lax.div(order_pos, 16)
    ).astype(BF)
    for p in range(3):
        lanes = ct_all[:, :, p * 256 : p * 256 + 256].reshape(128, 256)
        both = dot_nt(order, lanes).astype(BF)
        cs[p, 0] = both[:256]
        cs[p, 1] = both[256:]
        cc[p] = jnp.concatenate([both[:256], earlier(both[:256])], axis=1)

    def grad_b_rows(into, first, planes, cots):
        lhs = jnp.concatenate(
            [jnp.concatenate([ht[plane, b] for b in range(3)], axis=0) for plane in planes], axis=1
        )
        rhs = jnp.concatenate([cc[p] for p in cots], axis=0)
        acc = dot(lhs, rhs)
        for b in range(3):
            block = acc[b * 128 : b * 128 + 128]
            pieces = (block[64:, 128:], block[:64, :128], block[64:, :128])
            for c in range(3):
                start = first + b * 24 + c * 8
                into[:, start : start + 8, :] = pieces[c].reshape(8, 8, 128)

    grad_b_rows(ge_f, 0, (1, 3), (1, 2))
    grad_b_rows(ge_f, 72, (1, 3), (0, 1))
    ge_f[:, 144:160, :] = jnp.zeros((8, 16, 128), F32)

    def halves(full, size, other):
        theirs = pl.ds(pl.multiple_of((1 - core) * size, 8), size)
        other[...] = full[:, theirs, :].astype(BF)

    def join(full, size, came, mine):
        own = pl.ds(pl.multiple_of(core * size, 8), size)
        mine[...] = (full[:, own, :] + came[...].astype(F32)).astype(BF)

    halves(ge_f, ROWS_E, ge_s)
    e0_copy().start()

    kc_copy(1 - core).wait_recv()

    @pl.loop(0, 8)
    def _(e):
        kb_f[e, 0:HALF] = kb_all[0, e].astype(F32)
        kb_f[e, HALF : 2 * HALF] = kb_all[1, e].astype(F32)

    @pl.loop(0, 9)
    def _(ab):
        k0, k1, k2 = [
            kb_f[:, pl.ds(pl.multiple_of(ab * 24 + c * 8, 8), 8), :].reshape(64, 128) for c in range(3)
        ]
        this = jnp.concatenate([k1, k2], axis=0)
        last = jnp.concatenate([jnp.zeros((64, 128), F32), k0], axis=0)
        wb[ab] = jnp.concatenate([this, last], axis=1).astype(BF)
        vb[ab] = jnp.concatenate([this.T, last.T], axis=1).astype(BF)

    e0_copy().wait_recv()
    join(ge_f, ROWS_E, ge_0, ge_h)
    others(SLABS, mp, lambda i: e1_copy(i, mp).start())
    ge_1[mp] = ge_h[mp]

    def slope(depth, rh, back):
        delta = back * jnp.where(pf[depth, rh] > 0, 1.0, 0.3)
        dd[depth, rh] = jnp.concatenate([delta, earlier(delta)], axis=1).astype(BF)

    for depth in range(2):
        for rd in range(2):
            for rh in range(2):
                along = [(1, 0)] if rd == 0 else [(2, 0), (0, 1)]
                down = [(1, 0)] if rh == 0 else [(2, 0), (0, 1)]
                lhs = [cs[depth + ahead, low] for _, ahead in along for _, low in down]
                rhs = [vb[a * 3 + b] for a, _ in along for b, _ in down]
                both = dot(jnp.concatenate(lhs, axis=1), jnp.concatenate(rhs, axis=0))
                back = (both[:, :128] + earlier(both[:, 128:])).astype(BF).astype(F32)
                if depth == 0 and rd == 0:
                    bk[rh] = back
                else:
                    slope(2 * depth + rd, rh, back)

    def grad_a_dot(a, depths):
        lhs = jnp.concatenate(
            [
                jnp.concatenate([xt[2 * depth + a, 2 * rh + b] for b in range(3)], axis=0)
                for depth in depths
                for rh in range(2)
            ],
            axis=1,
        )
        rhs = dd[depths[0] : depths[-1] + 1].reshape(512 * len(depths), 256)
        return dot(lhs, rhs)

    @pl.loop(0, 3)
    def _(a):
        acc_a[a] = grad_a_dot(a, (1, 2, 3))

    @pl.when(mp > 0)
    def _():
        x_halo().wait_recv()

    @pl.when(mp == 0)
    def _():
        xv[0] = jnp.zeros((64, 2048), BF)

    prepare(0)
    convolve(0)
    turn_x(0)
    for rh in range(2):
        slope(0, rh, bk[rh])

    lane = lax.broadcasted_iota(jnp.int32, (16, 128), 1)

    @pl.loop(0, 3)
    def _(a):
        acc = acc_a[a] + grad_a_dot(a, (0,))
        for b in range(3):
            this = acc[b * 128 : b * 128 + 128, :128]
            last = acc[b * 128 + 96 : b * 128 + 128, 128:]
            turned = pltpu.roll(this, 64, 1)
            sums = (last + turned[32:64], this[0:32] + turned[64:96], this[32:64] + turned[96:128])
            for c in range(3):
                packed = jnp.where(lane < 64, sums[c][:16], pltpu.roll(sums[c][16:], 64, 1))
                ga_f[pl.ds(pl.multiple_of(a * 144 + b * 48 + c * 16, 16), 16), :] = packed

    ga_f[432:512, :] = jnp.zeros((80, 128), F32)
    ga_s[...] = ga_f[...].reshape(GROUP, ROWS_A, 128).astype(BF)
    others(GROUP, me, lambda i: a1_copy(i, me).start())
    ga_1[me] = ga_s[me]

    turn_h(0)
    grad_b_rows(gl_f, 0, (0, 2), (0, 1))
    gl_f[:, 72:96, :] = jnp.zeros((8, 24, 128), F32)
    halves(gl_f, ROWS_L, gl_s)
    l0_copy().start()
    def features_of(into, place, terms):
        lhs = [hs[p, b] for p, _ in terms for b in range(3)]
        rhs = [wb[a * 3 + b] for _, a in terms for b in range(3)]
        both = dot(jnp.concatenate(lhs, axis=1), jnp.concatenate(rhs, axis=0))
        out = (both[:, :128] + later(both[:, 128:])).astype(BF)
        turned = dot_tn(out, order[:256]).astype(BF)
        into[:, :, place : place + 256] = turned.reshape(8, 16, 256)

    features_of(ft_up, 0, [(1, 0), (2, 1), (3, 2)])
    features_of(ft_up, 256, [(3, 0)])
    others(SLABS, mp, lambda i: fu_copy(i, mp).start())
    fr_up[mp] = ft_up[mp]
    features_of(ft_low, 0, [(0, 1), (1, 2)])
    others(SLABS, mp, lambda i: fl_copy(i, mp).start())
    fr_low[mp] = ft_low[mp]
    others(SLABS, mp, lambda i: e1_copy(i, i).wait_recv())
    ge_2s[...] = jnp.sum(ge_1[...].astype(F32), axis=0).astype(BF)
    others(ring, rank, lambda i: e2_copy(i, rank).start())
    ge_2[rank] = ge_2s[...]
    l0_copy().wait_recv()
    join(gl_f, ROWS_L, gl_0, gl_h)
    others(SLABS, mp, lambda i: l1_copy(i, mp).start())
    gl_1[mp] = gl_h[mp]

    others(GROUP, me, lambda i: a1_copy(i, i).wait_recv())
    ga_2s[...] = jnp.sum(ga_1[...].astype(F32), axis=0)
    others(ring, rank, lambda i: a2_copy(i, rank).start())
    ga_2[rank] = ga_2s[...]

    others(ring, rank, lambda i: e2_copy(i, i).wait_recv())
    ge_3[core] = jnp.sum(ge_2[...].astype(F32), axis=0) * scale_b
    e3_copy(core).start()

    others(SLABS, mp, lambda i: l1_copy(i, i).wait_recv())
    gl_2s[...] = jnp.sum(gl_1[...].astype(F32), axis=0).astype(BF)
    others(ring, rank, lambda i: l2_copy(i, rank).start())
    gl_2[rank] = gl_2s[...]

    others(ring, rank, lambda i: a2_copy(i, i).wait_recv())
    ga_3s[...] = (jnp.sum(ga_2[...], axis=0) * scale_a).astype(BF)
    others(GROUP, me, lambda i: a3_copy(i, me).start())
    ga_3[me] = ga_3s[...]

    others(SLABS, mp, lambda i: fu_copy(i, i).wait_recv())
    others(SLABS, mp, lambda i: fl_copy(i, i).wait_recv())
    for e in range(SLABS):
        first = fr_low[e].astype(F32)
        if e > 0:
            first = first + fr_up[e - 1, :, 256:512].astype(F32)
        planes = jnp.concatenate([first.astype(BF), fr_up[e, :, 0:256]], axis=1)
        feat[e * 512 : e * 512 + 512, :] = dot_tn(planes, eye).astype(BF)

    e3_copy(1 - core).wait_recv()
    gbe[...] = ge_3[...]
    others(ring, rank, lambda i: l2_copy(i, i).wait_recv())
    gl_3[core] = jnp.sum(gl_2[...].astype(F32), axis=0) * scale_b
    l3_copy(core).start()

    @pl.when(mp < SLABS - 1)
    def _():
        x_halo().wait_send()

    others(SLABS, mp, lambda i: kb_copy(i, mp).wait_send())
    kc_copy(core).wait_send()
    others(SLABS, mp, lambda i: ct_copy(i, mp).wait_send())
    others(SLABS, mp, lambda i: fu_copy(i, mp).wait_send())
    others(SLABS, mp, lambda i: fl_copy(i, mp).wait_send())
    e0_copy().wait_send()
    l0_copy().wait_send()
    others(SLABS, mp, lambda i: e1_copy(i, mp).wait_send())
    others(SLABS, mp, lambda i: l1_copy(i, mp).wait_send())
    others(ring, rank, lambda i: e2_copy(i, rank).wait_send())
    e3_copy(core).wait_send()
    others(ring, rank, lambda i: l2_copy(i, rank).wait_send())
    others(GROUP, me, lambda i: a1_copy(i, me).wait_send())
    others(ring, rank, lambda i: a2_copy(i, rank).wait_send())

    l3_copy(1 - core).wait_recv()
    gbl[...] = gl_3[...]
    l3_copy(core).wait_send()
    others(GROUP, me, lambda i: a3_copy(i, i).wait_recv())
    ga[...] = ga_3[...]
    others(GROUP, me, lambda i: a3_copy(i, me).wait_send())


def finish(feat_in, ga_in, gbe, gbl, feat, ga, gb, ga_v, sem):
    moves = [
        (feat_in, feat),
        (gbe.at[0, pl.ds(0, 72)], gb.at[pl.ds(0, 72)]),
        (gbl.at[0, pl.ds(0, 48)], gb.at[pl.ds(72, 48)]),
        (gbl.at[1, pl.ds(0, 24)], gb.at[pl.ds(120, 24)]),
        (gbe.at[0, pl.ds(72, 8)], gb.at[pl.ds(144, 8)]),
        (gbe.at[1, pl.ds(0, 64)], gb.at[pl.ds(152, 64)]),
        (ga_v, ga),
    ]
    copies = [pltpu.make_async_copy(src, dst, sem.at[place]) for place, (src, dst) in enumerate(moves)]
    for copy in copies[:-1]:
        copy.start()
    whole = ga_in[...].astype(F32).reshape(GROUP * ROWS_A, 128)[:432].reshape(27, 16, 128)
    ga_v[:, 0:16, :] = whole[:, :, :64]
    ga_v[:, 16:32, :] = whole[:, :, 64:]
    copies[-1].start()
    for copy in copies:
        copy.wait()


def hbm(array):
    return pltpu.with_memory_space_constraint(array, pltpu.HBM)


def shards(ring, samples, volume, kernel_a, kernel_b, cotangent):
    scale_a = 1.0 / math.sqrt(samples * 32**3)
    scale_b = 1.0 / math.sqrt(samples * 16**3)
    vmem = pltpu.VMEM
    dma = pltpu.SemaphoreType.DMA
    scratch = [
        vmem((9, 64, 2048), BF),
        vmem((9, 96, 64), BF),
        vmem((216, 128), BF),
        vmem((4096, 16), BF),
        vmem((9, 5, 256, 128), BF),
        vmem((9, 5, 128, 256), BF),
        vmem((9, 128, 256), BF),
        vmem((4, 2, 256, 128), F32),
        vmem((4, 3, 256, 128), BF),
        vmem((4, 3, 128, 256), BF),
        vmem((16, 4352), BF),
        vmem((8, 16, 768), BF),
        vmem((CORES, HALF, 128), BF),
        vmem((CORES, 8, HALF, 128), BF),
        vmem((8, 224, 128), F32),
        vmem((9, 128, 256), BF),
        vmem((9, 128, 256), BF),
        vmem((3, 2, 256, 128), BF),
        vmem((3, 256, 256), BF),
        vmem((8, 16, 512), BF),
        vmem((8, 16, 512), BF),
        vmem((8, 16, 256), BF),
        vmem((8, 16, 256), BF),
        vmem((4, 2, 256, 256), BF),
        vmem((2, 256, 128), F32),
        vmem((3, 384, 256), F32),
        vmem((8, 160, 128), F32),
        vmem((8, ROWS_E, 128), BF),
        vmem((8, ROWS_E, 128), BF),
        vmem((8, ROWS_E, 128), BF),
        vmem((8, ROWS_E, 128), BF),
        vmem((ROWS_E, 128), BF),
        vmem((ring, ROWS_E, 128), BF),
        vmem((CORES, ROWS_E, 128), F32),
        vmem((8, 96, 128), F32),
        vmem((8, ROWS_L, 128), BF),
        vmem((8, ROWS_L, 128), BF),
        vmem((8, ROWS_L, 128), BF),
        vmem((8, ROWS_L, 128), BF),
        vmem((ROWS_L, 128), BF),
        vmem((ring, ROWS_L, 128), BF),
        vmem((CORES, ROWS_L, 128), F32),
        vmem((512, 128), F32),
        vmem((GROUP, ROWS_A, 128), BF),
        vmem((GROUP, ROWS_A, 128), BF),
        vmem((ROWS_A, 128), F32),
        vmem((ring, ROWS_A, 128), F32),
        vmem((ROWS_A, 128), BF),
        vmem((GROUP, ROWS_A, 128), BF),
        dma((8,)),
        dma((3,)),
        dma,
        dma,
        dma((8,)),
        dma((8,)),
        dma((8,)),
        dma((8,)),
        dma,
        dma,
        dma((8,)),
        dma((8,)),
        dma((8,)),
        dma((8,)),
        dma,
        dma,
        dma((8,)),
        dma((8,)),
        dma((ring,)),
        dma((ring,)),
        dma,
        dma,
        dma,
        dma,
        dma((8,)),
        dma((8,)),
        dma((ring,)),
        dma((ring,)),
        dma,
        dma,
        dma((GROUP,)),
        dma((GROUP,)),
        dma((ring,)),
        dma((ring,)),
        dma((GROUP,)),
        dma((GROUP,)),
    ]
    in_vmem = pl.BlockSpec(memory_space=pltpu.VMEM)
    in_hbm = pl.BlockSpec(memory_space=pltpu.HBM)
    parts = pl.pallas_call(
        functools.partial(body, ring, scale_a, scale_b),
        out_shape=(
            jax.ShapeDtypeStruct((4096, 16), BF),
            jax.ShapeDtypeStruct((GROUP, ROWS_A, 128), BF),
            jax.ShapeDtypeStruct((CORES, ROWS_E, 128), F32),
            jax.ShapeDtypeStruct((CORES, ROWS_L, 128), F32),
        ),
        in_specs=[in_hbm] * 4,
        out_specs=(in_vmem,) * 4,
        scratch_shapes=scratch,
        compiler_params=pltpu.CompilerParams(
            collective_id=0, has_side_effects=True, vmem_limit_bytes=48 * 1024 * 1024
        ),
        cost_estimate=pl.CostEstimate(flops=1600000000, bytes_accessed=4000000, transcendentals=0),
    )(
        hbm(volume.reshape(8, 64, 2048)),
        hbm(kernel_a.reshape(9, 96, 64)),
        hbm(kernel_b.reshape(216, 128)),
        hbm(cotangent.reshape(4096, 16)),
    )
    feat, ga, gb = pl.pallas_call(
        finish,
        out_shape=(
            jax.ShapeDtypeStruct((4096, 16), BF),
            jax.ShapeDtypeStruct((27, 32, 64), F32),
            jax.ShapeDtypeStruct((216, 128), F32),
        ),
        in_specs=[in_vmem] * 4,
        out_specs=(in_hbm, in_hbm, in_hbm),
        scratch_shapes=[vmem((27, 32, 64), F32), dma((7,))],
        compiler_params=pltpu.CompilerParams(vmem_limit_bytes=4 * 1024 * 1024),
    )(*parts)
    return (
        feat.reshape(1, 16, 16, 16, 16),
        ga.reshape(3, 3, 3, 32, 64),
        gb.reshape(3, 3, 3, 8, 128),
    )


def solution(mesh):
    ring = mesh.shape["dp"] // CORES
    return jax.shard_map(
        functools.partial(shards, ring, mesh.shape["dp"]),
        mesh=mesh,
        in_specs=(
            P("dp", "mp", None, None),
            P(),
            P(None, None, None, "mp", None),
            P("dp", None, None, None, "mp"),
        ),
        out_specs=(P("dp", None, None, None, "mp"), P(), P(None, None, None, "mp", None)),
        check_vma=False,
    )
```

time: 47.3 us -> 43.8 us (0.926)
  Pallas kernels: 46.5 us -> 43 us
    pallas_call x1, Pallas kernels: 44.1 us -> 41.8 us  [shards(): pl.pallas_call(functools.partial(body, ring, scale_a, scale_b), out_shape...]
    pallas_call x1, Pallas kernels: 2.42 us -> 1.21 us  [shards(): pl.pallas_call(finish, out_shape=(jax.ShapeDtypeStruct((4096, 16), BF), j...]
where the time goes in v3:
time: 43.8 us; the launch traced here: 43.7 us
  Pallas kernels  43 us (98%)
  between operations  0.64 us (1%)
    pallas_call x1, Pallas kernels, shards(): pl.pallas_call(functools.partial(body, ring, scale_a, scale_b), out_shape...  41.8 us
    pallas_call x1, Pallas kernels, shards(): pl.pallas_call(finish, out_shape=(jax.ShapeDtypeStruct((4096, 16), BF), j...  1.21 us

profile of v3, /device:TPU:1, one launch (start us, length us, event | category | flops | bytes accessed | tf_op | source)
XLA Modules:
  0.0 43.7 jit_solution(12747649161305384976)
XLA Ops:
  0.6 41.8 %shard_map.67 = (bf16[4096,16]{1,0:T(8,128)(2,1)S(1)}, bf16[16,32,128]{2,1,0:T(8,128)(2,1)S(1)}, f32[2,80,128]{2,1,0:T(8,128)S(1)}, f32[2,48,128]{2,1,0:T(8,128)S(1)}) custom-call(bf16[8,64,2048]{2,1,0:T(8,128)(2,1)} %bitcast.7, bf16[9,96,64]{2,1,0:T(8,128)(2,1)} %bitcast.11, bf16[216,128]{1,0:T(8,128)(2,1)} %bitcast.13, bf16[4096,16]{1,0:T(8,128)(2,1)} %bitcast.8), custom_call_target="tpu_custom_call" | custom-call | flops 1600000000 | bytes 4000000 | tf_op jit(solution)/shard_map/pallas_call | solution.py:686
  42.5 1.2 %shard_map.68 = (bf16[4096,16]{1,0:T(8,128)(2,1)}, f32[27,32,64]{2,1,0:T(8,128)}, f32[216,128]{1,0:T(8,128)}) custom-call(bf16[4096,16]{1,0:T(8,128)(2,1)S(1)} %get-tuple-element.10.feat_in, bf16[16,32,128]{2,1,0:T(8,128)(2,1)S(1)} %get-tuple-element.11.ga_in, f32[2,80,128]{2,1,0:T(8,128)S(1)} %get-tuple-element.12.gbe, f32[2,48,128]{2,1,0:T(8,128)S(1)} %get-tuple-element.13.gbl), custom_call_target="tpu_custom_call" | custom-call | tf_op jit(solution)/shard_map/pallas_call | solution.py:707

commit v4 on v3

--- a/solution.py
+++ b/solution.py
@@ -15,8 +15,6 @@
 CORES = 2
 GROUP = SLABS * CORES
 HALF = 112
-ROWS_E = 80
-ROWS_L = 48
 ROWS_A = 32
 
 
@@ -58,8 +56,7 @@
     cot_hbm,
     feat,
     ga,
-    gbe,
-    gbl,
+    gb,
     xv,
     ka,
     kb,
@@ -79,29 +76,19 @@
     vb,
     cs,
     cc,
-    ft_up,
-    fr_up,
-    ft_low,
-    fr_low,
+    ft,
+    fr,
     dd,
     bk,
     acc_a,
-    ge_f,
-    ge_s,
-    ge_0,
-    ge_h,
-    ge_1,
-    ge_2s,
-    ge_2,
-    ge_3,
-    gl_f,
-    gl_s,
-    gl_0,
-    gl_h,
-    gl_1,
-    gl_2s,
-    gl_2,
-    gl_3,
+    gb_f,
+    gb_s,
+    gb_0,
+    gb_h,
+    gb_1,
+    gb_2s,
+    gb_2,
+    gb_3,
     ga_f,
     ga_s,
     ga_1,
@@ -119,26 +106,16 @@
     kb_recv,
     kc_send,
     kc_recv,
-    fu_send,
-    fu_recv,
-    fl_send,
-    fl_recv,
-    e0_send,
-    e0_recv,
-    e1_send,
-    e1_recv,
-    e2_send,
-    e2_recv,
-    e3_send,
-    e3_recv,
-    l0_send,
-    l0_recv,
-    l1_send,
-    l1_recv,
-    l2_send,
-    l2_recv,
-    l3_send,
-    l3_recv,
+    ft_send,
+    ft_recv,
+    b0_send,
+    b0_recv,
+    b1_send,
+    b1_recv,
+    b2_send,
+    b2_recv,
+    b3_send,
+    b3_recv,
     a1_send,
     a1_recv,
     a2_send,
@@ -265,35 +242,20 @@
     def kc_copy(half):
         return remote(kb_all.at[half], kb_all.at[half], kc_send, kc_recv, in_group(mp * CORES + 1 - core))
 
-    def fu_copy(peer, slot):
-        return remote(ft_up.at[peer], fr_up.at[slot], fu_send.at[peer], fu_recv.at[slot], in_slabs(peer))
-
-    def fl_copy(peer, slot):
-        return remote(ft_low.at[peer], fr_low.at[slot], fl_send.at[peer], fl_recv.at[slot], in_slabs(peer))
-
-    def e0_copy():
-        return remote(ge_s, ge_0, e0_send, e0_recv, in_group(mp * CORES + 1 - core))
-
-    def e1_copy(peer, slot):
-        return remote(ge_h.at[peer], ge_1.at[slot], e1_send.at[peer], e1_recv.at[slot], in_slabs(peer))
-
-    def e2_copy(peer, slot):
-        return remote(ge_2s, ge_2.at[slot], e2_send.at[peer], e2_recv.at[slot], in_ring(peer))
-
-    def e3_copy(slot):
-        return remote(ge_3.at[core], ge_3.at[slot], e3_send, e3_recv, in_group(mp * CORES + 1 - core))
-
-    def l0_copy():
-        return remote(gl_s, gl_0, l0_send, l0_recv, in_group(mp * CORES + 1 - core))
-
-    def l1_copy(peer, slot):
-        return remote(gl_h.at[peer], gl_1.at[slot], l1_send.at[peer], l1_recv.at[slot], in_slabs(peer))
-
-    def l2_copy(peer, slot):
-        return remote(gl_2s, gl_2.at[slot], l2_send.at[peer], l2_recv.at[slot], in_ring(peer))
-
-    def l3_copy(slot):
-        return remote(gl_3.at[core], gl_3.at[slot], l3_send, l3_recv, in_group(mp * CORES + 1 - core))
+    def ft_copy(peer, slot):
+        return remote(ft.at[peer], fr.at[slot], ft_send.at[peer], ft_recv.at[slot], in_slabs(peer))
+
+    def b0_copy():
+        return remote(gb_s, gb_0, b0_send, b0_recv, in_group(mp * CORES + 1 - core))
+
+    def b1_copy(peer, slot):
+        return remote(gb_h.at[peer], gb_1.at[slot], b1_send.at[peer], b1_recv.at[slot], in_slabs(peer))
+
+    def b2_copy(peer, slot):
+        return remote(gb_2s, gb_2.at[slot], b2_send.at[peer], b2_recv.at[slot], in_ring(peer))
+
+    def b3_copy(slot):
+        return remote(gb_3.at[core], gb_3.at[slot], b3_send, b3_recv, in_group(mp * CORES + 1 - core))
 
     def a1_copy(peer, slot):
         return remote(ga_s.at[peer], ga_1.at[slot], a1_send.at[peer], a1_recv.at[slot], in_group(peer))
@@ -336,12 +298,25 @@
     def _(index):
         turn_x(index)
 
-    @pl.loop(1, 4)
-    def _(index):
-        turn_h(index)
-
     others(SLABS, mp, lambda i: kb_copy(i, i).wait_recv())
     kc_copy(core).start()
+
+    kc_copy(1 - core).wait_recv()
+
+    @pl.loop(0, 8)
+    def _(e):
+        kb_f[e, 0:HALF] = kb_all[0, e].astype(F32)
+        kb_f[e, HALF : 2 * HALF] = kb_all[1, e].astype(F32)
+
+    @pl.loop(0, 9)
+    def _(ab):
+        k0, k1, k2 = [
+            kb_f[:, pl.ds(pl.multiple_of(ab * 24 + c * 8, 8), 8), :].reshape(64, 128) for c in range(3)
+        ]
+        this = jnp.concatenate([k1, k2], axis=0)
+        last = jnp.concatenate([jnp.zeros((64, 128), F32), k0], axis=0)
+        wb[ab] = jnp.concatenate([this, last], axis=1).astype(BF)
+        vb[ab] = jnp.concatenate([this.T, last.T], axis=1).astype(BF)
 
     others(SLABS, mp, lambda i: ct_copy(i, i).wait_recv())
     order_row = lax.broadcasted_iota(jnp.int32, (512, 256), 0)
@@ -357,56 +332,6 @@
         cs[p, 1] = both[256:]
         cc[p] = jnp.concatenate([both[:256], earlier(both[:256])], axis=1)
 
-    def grad_b_rows(into, first, planes, cots):
-        lhs = jnp.concatenate(
-            [jnp.concatenate([ht[plane, b] for b in range(3)], axis=0) for plane in planes], axis=1
-        )
-        rhs = jnp.concatenate([cc[p] for p in cots], axis=0)
-        acc = dot(lhs, rhs)
-        for b in range(3):
-            block = acc[b * 128 : b * 128 + 128]
-            pieces = (block[64:, 128:], block[:64, :128], block[64:, :128])
-            for c in range(3):
-                start = first + b * 24 + c * 8
-                into[:, start : start + 8, :] = pieces[c].reshape(8, 8, 128)
-
-    grad_b_rows(ge_f, 0, (1, 3), (1, 2))
-    grad_b_rows(ge_f, 72, (1, 3), (0, 1))
-    ge_f[:, 144:160, :] = jnp.zeros((8, 16, 128), F32)
-
-    def halves(full, size, other):
-        theirs = pl.ds(pl.multiple_of((1 - core) * size, 8), size)
-        other[...] = full[:, theirs, :].astype(BF)
-
-    def join(full, size, came, mine):
-        own = pl.ds(pl.multiple_of(core * size, 8), size)
-        mine[...] = (full[:, own, :] + came[...].astype(F32)).astype(BF)
-
-    halves(ge_f, ROWS_E, ge_s)
-    e0_copy().start()
-
-    kc_copy(1 - core).wait_recv()
-
-    @pl.loop(0, 8)
-    def _(e):
-        kb_f[e, 0:HALF] = kb_all[0, e].astype(F32)
-        kb_f[e, HALF : 2 * HALF] = kb_all[1, e].astype(F32)
-
-    @pl.loop(0, 9)
-    def _(ab):
-        k0, k1, k2 = [
-            kb_f[:, pl.ds(pl.multiple_of(ab * 24 + c * 8, 8), 8), :].reshape(64, 128) for c in range(3)
-        ]
-        this = jnp.concatenate([k1, k2], axis=0)
-        last = jnp.concatenate([jnp.zeros((64, 128), F32), k0], axis=0)
-        wb[ab] = jnp.concatenate([this, last], axis=1).astype(BF)
-        vb[ab] = jnp.concatenate([this.T, last.T], axis=1).astype(BF)
-
-    e0_copy().wait_recv()
-    join(ge_f, ROWS_E, ge_0, ge_h)
-    others(SLABS, mp, lambda i: e1_copy(i, mp).start())
-    ge_1[mp] = ge_h[mp]
-
     def slope(depth, rh, back):
         delta = back * jnp.where(pf[depth, rh] > 0, 1.0, 0.3)
         dd[depth, rh] = jnp.concatenate([delta, earlier(delta)], axis=1).astype(BF)
@@ -474,68 +399,75 @@
     others(GROUP, me, lambda i: a1_copy(i, me).start())
     ga_1[me] = ga_s[me]
 
-    turn_h(0)
-    grad_b_rows(gl_f, 0, (0, 2), (0, 1))
-    gl_f[:, 72:96, :] = jnp.zeros((8, 24, 128), F32)
-    halves(gl_f, ROWS_L, gl_s)
-    l0_copy().start()
-    def features_of(into, place, terms):
+    def grad_b_rows(a, planes, cots):
+        lhs = jnp.concatenate(
+            [jnp.concatenate([ht[plane, b] for b in range(3)], axis=0) for plane in planes], axis=1
+        )
+        rhs = jnp.concatenate([cc[p] for p in cots], axis=0)
+        acc = dot(lhs, rhs)
+        for b in range(3):
+            block = acc[b * 128 : b * 128 + 128]
+            pieces = (block[64:, 128:], block[:64, :128], block[64:, :128])
+            for c in range(3):
+                start = a * 72 + b * 24 + c * 8
+                gb_f[:, start : start + 8, :] = pieces[c].reshape(8, 8, 128)
+
+    @pl.loop(0, 4)
+    def _(index):
+        turn_h(index)
+
+    grad_b_rows(0, (1, 3), (1, 2))
+    grad_b_rows(1, (0, 2), (0, 1))
+    grad_b_rows(2, (1, 3), (0, 1))
+    gb_f[:, 216:224, :] = jnp.zeros((8, 8, 128), F32)
+    gb_s[...] = gb_f[:, pl.ds(pl.multiple_of((1 - core) * HALF, 8), HALF), :].astype(BF)
+    b0_copy().start()
+
+    def features_of(plane, terms):
         lhs = [hs[p, b] for p, _ in terms for b in range(3)]
         rhs = [wb[a * 3 + b] for _, a in terms for b in range(3)]
         both = dot(jnp.concatenate(lhs, axis=1), jnp.concatenate(rhs, axis=0))
         out = (both[:, :128] + later(both[:, 128:])).astype(BF)
         turned = dot_tn(out, order[:256]).astype(BF)
-        into[:, :, place : place + 256] = turned.reshape(8, 16, 256)
-
-    features_of(ft_up, 0, [(1, 0), (2, 1), (3, 2)])
-    features_of(ft_up, 256, [(3, 0)])
-    others(SLABS, mp, lambda i: fu_copy(i, mp).start())
-    fr_up[mp] = ft_up[mp]
-    features_of(ft_low, 0, [(0, 1), (1, 2)])
-    others(SLABS, mp, lambda i: fl_copy(i, mp).start())
-    fr_low[mp] = ft_low[mp]
-    others(SLABS, mp, lambda i: e1_copy(i, i).wait_recv())
-    ge_2s[...] = jnp.sum(ge_1[...].astype(F32), axis=0).astype(BF)
-    others(ring, rank, lambda i: e2_copy(i, rank).start())
-    ge_2[rank] = ge_2s[...]
-    l0_copy().wait_recv()
-    join(gl_f, ROWS_L, gl_0, gl_h)
-    others(SLABS, mp, lambda i: l1_copy(i, mp).start())
-    gl_1[mp] = gl_h[mp]
+        ft[:, :, plane * 256 : plane * 256 + 256] = turned.reshape(8, 16, 256)
+
+    features_of(0, [(0, 1), (1, 2)])
+    b0_copy().wait_recv()
+    own = pl.ds(pl.multiple_of(core * HALF, 8), HALF)
+    gb_h[...] = (gb_f[:, own, :] + gb_0[...].astype(F32)).astype(BF)
+    others(SLABS, mp, lambda i: b1_copy(i, mp).start())
+    gb_1[mp] = gb_h[mp]
+    features_of(1, [(1, 0), (2, 1), (3, 2)])
+    features_of(2, [(3, 0)])
+    others(SLABS, mp, lambda i: ft_copy(i, mp).start())
+    fr[mp] = ft[mp]
 
     others(GROUP, me, lambda i: a1_copy(i, i).wait_recv())
     ga_2s[...] = jnp.sum(ga_1[...].astype(F32), axis=0)
     others(ring, rank, lambda i: a2_copy(i, rank).start())
     ga_2[rank] = ga_2s[...]
 
-    others(ring, rank, lambda i: e2_copy(i, i).wait_recv())
-    ge_3[core] = jnp.sum(ge_2[...].astype(F32), axis=0) * scale_b
-    e3_copy(core).start()
-
-    others(SLABS, mp, lambda i: l1_copy(i, i).wait_recv())
-    gl_2s[...] = jnp.sum(gl_1[...].astype(F32), axis=0).astype(BF)
-    others(ring, rank, lambda i: l2_copy(i, rank).start())
-    gl_2[rank] = gl_2s[...]
+    others(SLABS, mp, lambda i: b1_copy(i, i).wait_recv())
+    gb_2s[...] = jnp.sum(gb_1[...].astype(F32), axis=0).astype(BF)
+    others(ring, rank, lambda i: b2_copy(i, rank).start())
+    gb_2[rank] = gb_2s[...]
 
     others(ring, rank, lambda i: a2_copy(i, i).wait_recv())
     ga_3s[...] = (jnp.sum(ga_2[...], axis=0) * scale_a).astype(BF)
     others(GROUP, me, lambda i: a3_copy(i, me).start())
     ga_3[me] = ga_3s[...]
 
-    others(SLABS, mp, lambda i: fu_copy(i, i).wait_recv())
-    others(SLABS, mp, lambda i: fl_copy(i, i).wait_recv())
+    others(SLABS, mp, lambda i: ft_copy(i, i).wait_recv())
     for e in range(SLABS):
-        first = fr_low[e].astype(F32)
+        first = fr[e, :, 0:256].astype(F32)
         if e > 0:
-            first = first + fr_up[e - 1, :, 256:512].astype(F32)
-        planes = jnp.concatenate([first.astype(BF), fr_up[e, :, 0:256]], axis=1)
+            first = first + fr[e - 1, :, 512:768].astype(F32)
+        planes = jnp.concatenate([first.astype(BF), fr[e, :, 256:512]], axis=1)
         feat[e * 512 : e * 512 + 512, :] = dot_tn(planes, eye).astype(BF)
 
-    e3_copy(1 - core).wait_recv()
-    gbe[...] = ge_3[...]
-    others(ring, rank, lambda i: l2_copy(i, i).wait_recv())
-    gl_3[core] = jnp.sum(gl_2[...].astype(F32), axis=0) * scale_b
-    l3_copy(core).start()
+    others(ring, rank, lambda i: b2_copy(i, i).wait_recv())
+    gb_3[core] = jnp.sum(gb_2[...].astype(F32), axis=0) * scale_b
+    b3_copy(core).start()
 
     @pl.when(mp < SLABS - 1)
     def _():
@@ -544,34 +476,27 @@
     others(SLABS, mp, lambda i: kb_copy(i, mp).wait_send())
     kc_copy(core).wait_send()
     others(SLABS, mp, lambda i: ct_copy(i, mp).wait_send())
-    others(SLABS, mp, lambda i: fu_copy(i, mp).wait_send())
-    others(SLABS, mp, lambda i: fl_copy(i, mp).wait_send())
-    e0_copy().wait_send()
-    l0_copy().wait_send()
-    others(SLABS, mp, lambda i: e1_copy(i, mp).wait_send())
-    others(SLABS, mp, lambda i: l1_copy(i, mp).wait_send())
-    others(ring, rank, lambda i: e2_copy(i, rank).wait_send())
-    e3_copy(core).wait_send()
-    others(ring, rank, lambda i: l2_copy(i, rank).wait_send())
+    others(SLABS, mp, lambda i: ft_copy(i, mp).wait_send())
+    b0_copy().wait_send()
+    others(SLABS, mp, lambda i: b1_copy(i, mp).wait_send())
+    others(ring, rank, lambda i: b2_copy(i, rank).wait_send())
     others(GROUP, me, lambda i: a1_copy(i, me).wait_send())
     others(ring, rank, lambda i: a2_copy(i, rank).wait_send())
 
-    l3_copy(1 - core).wait_recv()
-    gbl[...] = gl_3[...]
-    l3_copy(core).wait_send()
+    b3_copy(1 - core).wait_recv()
+    gb[...] = gb_3[...]
+    b3_copy(core).wait_send()
     others(GROUP, me, lambda i: a3_copy(i, i).wait_recv())
     ga[...] = ga_3[...]
     others(GROUP, me, lambda i: a3_copy(i, me).wait_send())
 
 
-def finish(feat_in, ga_in, gbe, gbl, feat, ga, gb, ga_v, sem):
+def finish(feat_in, ga_in, gb_in, feat, ga, gb, ga_v, sem):
+    rest = 216 - HALF
     moves = [
         (feat_in, feat),
-        (gbe.at[0, pl.ds(0, 72)], gb.at[pl.ds(0, 72)]),
-        (gbl.at[0, pl.ds(0, 48)], gb.at[pl.ds(72, 48)]),
-        (gbl.at[1, pl.ds(0, 24)], gb.at[pl.ds(120, 24)]),
-        (gbe.at[0, pl.ds(72, 8)], gb.at[pl.ds(144, 8)]),
-        (gbe.at[1, pl.ds(0, 64)], gb.at[pl.ds(152, 64)]),
+        (gb_in.at[0], gb.at[pl.ds(0, HALF)]),
+        (gb_in.at[1, pl.ds(0, rest)], gb.at[pl.ds(HALF, rest)]),
         (ga_v, ga),
     ]
     copies = [pltpu.make_async_copy(src, dst, sem.at[place]) for place, (src, dst) in enumerate(moves)]
@@ -614,29 +539,19 @@
         vmem((9, 128, 256), BF),
         vmem((3, 2, 256, 128), BF),
         vmem((3, 256, 256), BF),
-        vmem((8, 16, 512), BF),
-        vmem((8, 16, 512), BF),
-        vmem((8, 16, 256), BF),
-        vmem((8, 16, 256), BF),
+        vmem((8, 16, 768), BF),
+        vmem((8, 16, 768), BF),
         vmem((4, 2, 256, 256), BF),
         vmem((2, 256, 128), F32),
         vmem((3, 384, 256), F32),
-        vmem((8, 160, 128), F32),
-        vmem((8, ROWS_E, 128), BF),
-        vmem((8, ROWS_E, 128), BF),
-        vmem((8, ROWS_E, 128), BF),
-        vmem((8, ROWS_E, 128), BF),
-        vmem((ROWS_E, 128), BF),
-        vmem((ring, ROWS_E, 128), BF),
-        vmem((CORES, ROWS_E, 128), F32),
-        vmem((8, 96, 128), F32),
-        vmem((8, ROWS_L, 128), BF),
-        vmem((8, ROWS_L, 128), BF),
-        vmem((8, ROWS_L, 128), BF),
-        vmem((8, ROWS_L, 128), BF),
-        vmem((ROWS_L, 128), BF),
-        vmem((ring, ROWS_L, 128), BF),
-        vmem((CORES, ROWS_L, 128), F32),
+        vmem((8, 224, 128), F32),
+        vmem((8, HALF, 128), BF),
+        vmem((8, HALF, 128), BF),
+        vmem((8, HALF, 128), BF),
+        vmem((8, HALF, 128), BF),
+        vmem((HALF, 128), BF),
+        vmem((ring, HALF, 128), BF),
+        vmem((CORES, HALF, 128), F32),
         vmem((512, 128), F32),
         vmem((GROUP, ROWS_A, 128), BF),
         vmem((GROUP, ROWS_A, 128), BF),
@@ -656,16 +571,6 @@
         dma,
         dma((8,)),
         dma((8,)),
-        dma((8,)),
-        dma((8,)),
-        dma,
-        dma,
-        dma((8,)),
-        dma((8,)),
-        dma((ring,)),
-        dma((ring,)),
-        dma,
-        dma,
         dma,
         dma,
         dma((8,)),
@@ -688,11 +593,10 @@
         out_shape=(
             jax.ShapeDtypeStruct((4096, 16), BF),
             jax.ShapeDtypeStruct((GROUP, ROWS_A, 128), BF),
-            jax.ShapeDtypeStruct((CORES, ROWS_E, 128), F32),
-            jax.ShapeDtypeStruct((CORES, ROWS_L, 128), F32),
+            jax.ShapeDtypeStruct((CORES, HALF, 128), F32),
         ),
         in_specs=[in_hbm] * 4,
-        out_specs=(in_vmem,) * 4,
+        out_specs=(in_vmem,) * 3,
         scratch_shapes=scratch,
         compiler_params=pltpu.CompilerParams(
             collective_id=0, has_side_effects=True, vmem_limit_bytes=48 * 1024 * 1024
@@ -711,9 +615,9 @@
             jax.ShapeDtypeStruct((27, 32, 64), F32),
             jax.ShapeDtypeStruct((216, 128), F32),
         ),
-        in_specs=[in_vmem] * 4,
+        in_specs=[in_vmem] * 3,
         out_specs=(in_hbm, in_hbm, in_hbm),
-        scratch_shapes=[vmem((27, 32, 64), F32), dma((7,))],
+        scratch_shapes=[vmem((27, 32, 64), F32), dma((4,))],
         compiler_params=pltpu.CompilerParams(vmem_limit_bytes=4 * 1024 * 1024),
     )(*parts)
     return (

time: 43.8 us -> 42.4 us (0.968)
  Pallas kernels: 43 us -> 41.6 us
    pallas_call x1, Pallas kernels: 41.8 us -> 40.4 us  [shards(): pl.pallas_call(functools.partial(body, ring, scale_a, scale_b), out_shape...]
where the time goes in v4:
time: 42.4 us; the launch traced here: 42.2 us
  Pallas kernels  41.6 us (98%)
  between operations  0.64 us (2%)
    pallas_call x1, Pallas kernels, shards(): pl.pallas_call(functools.partial(body, ring, scale_a, scale_b), out_shape...  40.4 us
    pallas_call x1, Pallas kernels, shards(): pl.pallas_call(finish, out_shape=(jax.ShapeDtypeStruct((4096, 16), BF), j...  1.18 us

profile of v4, /device:TPU:1, one launch (start us, length us, event | category | flops | bytes accessed | tf_op | source)
XLA Modules:
  0.0 42.2 jit_solution(8626561022920941425)
XLA Ops:
  0.6 40.4 %shard_map.67 = (bf16[4096,16]{1,0:T(8,128)(2,1)S(1)}, bf16[16,32,128]{2,1,0:T(8,128)(2,1)S(1)}, f32[2,112,128]{2,1,0:T(8,128)S(1)}) custom-call(bf16[8,64,2048]{2,1,0:T(8,128)(2,1)} %bitcast.7, bf16[9,96,64]{2,1,0:T(8,128)(2,1)} %bitcast.11, bf16[216,128]{1,0:T(8,128)(2,1)} %bitcast.13, bf16[4096,16]{1,0:T(8,128)(2,1)} %bitcast.8), custom_call_target="tpu_custom_call" | custom-call | flops 1600000000 | bytes 4000000 | tf_op jit(solution)/shard_map/pallas_call | solution.py:591
  41.1 1.2 %shard_map.68 = (bf16[4096,16]{1,0:T(8,128)(2,1)}, f32[27,32,64]{2,1,0:T(8,128)}, f32[216,128]{1,0:T(8,128)}) custom-call(bf16[4096,16]{1,0:T(8,128)(2,1)S(1)} %get-tuple-element.9.feat_in, bf16[16,32,128]{2,1,0:T(8,128)(2,1)S(1)} %get-tuple-element.10.ga_in, f32[2,112,128]{2,1,0:T(8,128)S(1)} %get-tuple-element.11.gb_in), custom_call_target="tpu_custom_call" | custom-call | tf_op jit(solution)/shard_map/pallas_call | solution.py:611

commit v5 on v4

--- a/solution.py
+++ b/solution.py
@@ -81,6 +81,7 @@
     dd,
     bk,
     acc_a,
+    acc_x,
     gb_f,
     gb_s,
     gb_0,
@@ -148,10 +149,6 @@
             src_ref=src, dst_ref=dst, send_sem=send, recv_sem=recv, device_id=device, device_id_type=MESH
         )
 
-    barrier = pltpu.get_barrier_semaphore()
-    others(GROUP, me, lambda i: pl.semaphore_signal(barrier, inc=1, device_id=in_group(i), device_id_type=MESH))
-    others(ring, rank, lambda i: pl.semaphore_signal(barrier, inc=1, device_id=in_ring(i), device_id_type=MESH))
-
     def plane_copy(plane):
         return pltpu.make_async_copy(x.at[plane], xv.at[plane + 1], x_sem.at[plane])
 
@@ -165,6 +162,10 @@
     @pl.loop(0, 8)
     def _(step):
         plane_copy(7 - step).start()
+
+    barrier = pltpu.get_barrier_semaphore()
+    others(GROUP, me, lambda i: pl.semaphore_signal(barrier, inc=1, device_id=in_group(i), device_id_type=MESH))
+    others(ring, rank, lambda i: pl.semaphore_signal(barrier, inc=1, device_id=in_ring(i), device_id_type=MESH))
 
     in_kb.wait()
     in_ka.wait()
@@ -206,11 +207,17 @@
             for q in range(16):
                 xs[index, s, q * 16 : q * 16 + 16, :] = rows[s * 16 : s * 16 + 16, q * 128 : q * 128 + 128]
 
-    def convolve(depth):
-        weights = wa[...].reshape(9 * 128, 256)
+    def conv_dot(depth, rh, offsets):
+        parts = [xs[2 * depth + a, 2 * rh + b] for a in offsets for b in range(3)]
+        weights = wa[3 * offsets[0] : 3 * offsets[-1] + 3].reshape(3 * len(offsets) * 128, 256)
+        return dot(jnp.concatenate(parts, axis=1), weights)
+
+    def convolve(depth, begun=None):
         for rh in range(2):
-            parts = [xs[2 * depth + a, 2 * rh + b] for a in range(3) for b in range(3)]
-            both = dot(jnp.concatenate(parts, axis=1), weights)
+            if begun is None:
+                both = conv_dot(depth, rh, (0, 1, 2))
+            else:
+                both = conv_dot(depth, rh, (0,)) + begun[rh]
             pre = both[:, :128] + later(both[:, 128:])
             pf[depth, rh] = pre
             hidden = jnp.where(pre > 0, pre, 0.3 * pre).astype(BF)
@@ -285,6 +292,8 @@
 
     plane_copy(0).wait()
     prepare(1)
+    for rh in range(2):
+        acc_x[rh] = conv_dot(0, rh, (1, 2))
 
     def turn_x(index):
         for s in range(5):
@@ -375,7 +384,7 @@
         xv[0] = jnp.zeros((64, 2048), BF)
 
     prepare(0)
-    convolve(0)
+    convolve(0, acc_x)
     turn_x(0)
     for rh in range(2):
         slope(0, rh, bk[rh])
@@ -457,6 +466,10 @@
     others(GROUP, me, lambda i: a3_copy(i, me).start())
     ga_3[me] = ga_3s[...]
 
+    others(ring, rank, lambda i: b2_copy(i, i).wait_recv())
+    gb_3[core] = jnp.sum(gb_2[...].astype(F32), axis=0) * scale_b
+    b3_copy(core).start()
+
     others(SLABS, mp, lambda i: ft_copy(i, i).wait_recv())
     for e in range(SLABS):
         first = fr[e, :, 0:256].astype(F32)
@@ -464,10 +477,6 @@
             first = first + fr[e - 1, :, 512:768].astype(F32)
         planes = jnp.concatenate([first.astype(BF), fr[e, :, 256:512]], axis=1)
         feat[e * 512 : e * 512 + 512, :] = dot_tn(planes, eye).astype(BF)
-
-    others(ring, rank, lambda i: b2_copy(i, i).wait_recv())
-    gb_3[core] = jnp.sum(gb_2[...].astype(F32), axis=0) * scale_b
-    b3_copy(core).start()
 
     @pl.when(mp < SLABS - 1)
     def _():
@@ -486,9 +495,9 @@
     b3_copy(1 - core).wait_recv()
     gb[...] = gb_3[...]
     b3_copy(core).wait_send()
+    others(GROUP, me, lambda i: a3_copy(i, me).wait_send())
     others(GROUP, me, lambda i: a3_copy(i, i).wait_recv())
     ga[...] = ga_3[...]
-    others(GROUP, me, lambda i: a3_copy(i, me).wait_send())
 
 
 def finish(feat_in, ga_in, gb_in, feat, ga, gb, ga_v, sem):
@@ -544,6 +553,7 @@
         vmem((4, 2, 256, 256), BF),
         vmem((2, 256, 128), F32),
         vmem((3, 384, 256), F32),
+        vmem((2, 256, 256), F32),
         vmem((8, 224, 128), F32),
         vmem((8, HALF, 128), BF),
         vmem((8, HALF, 128), BF),

time: 42.4 us -> 41.6 us (0.981)
  Pallas kernels: 41.6 us -> 40.9 us
    pallas_call x1, Pallas kernels: 40.4 us -> 39.7 us  [shards(): pl.pallas_call(functools.partial(body, ring, scale_a, scale_b), out_shape...]
where the time goes in v5:
time: 41.6 us; the launch traced here: 41.5 us
  Pallas kernels  40.9 us (98%)
  between operations  0.64 us (2%)
    pallas_call x1, Pallas kernels, shards(): pl.pallas_call(functools.partial(body, ring, scale_a, scale_b), out_shape...  39.7 us
    pallas_call x1, Pallas kernels, shards(): pl.pallas_call(finish, out_shape=(jax.ShapeDtypeStruct((4096, 16), BF), j...  1.18 us

profile of v5, /device:TPU:1, one launch (start us, length us, event | category | flops | bytes accessed | tf_op | source)
XLA Modules:
  0.0 41.5 jit_solution(13515426254919267563)
XLA Ops:
  0.6 39.7 %shard_map.67 = (bf16[4096,16]{1,0:T(8,128)(2,1)S(1)}, bf16[16,32,128]{2,1,0:T(8,128)(2,1)S(1)}, f32[2,112,128]{2,1,0:T(8,128)S(1)}) custom-call(bf16[8,64,2048]{2,1,0:T(8,128)(2,1)} %bitcast.7, bf16[9,96,64]{2,1,0:T(8,128)(2,1)} %bitcast.11, bf16[216,128]{1,0:T(8,128)(2,1)} %bitcast.13, bf16[4096,16]{1,0:T(8,128)(2,1)} %bitcast.8), custom_call_target="tpu_custom_call" | custom-call | flops 1600000000 | bytes 4000000 | tf_op jit(solution)/shard_map/pallas_call | solution.py:601
  40.3 1.2 %shard_map.68 = (bf16[4096,16]{1,0:T(8,128)(2,1)}, f32[27,32,64]{2,1,0:T(8,128)}, f32[216,128]{1,0:T(8,128)}) custom-call(bf16[4096,16]{1,0:T(8,128)(2,1)S(1)} %get-tuple-element.9.feat_in, bf16[16,32,128]{2,1,0:T(8,128)(2,1)S(1)} %get-tuple-element.10.ga_in, f32[2,112,128]{2,1,0:T(8,128)S(1)} %get-tuple-element.11.gb_in), custom_call_target="tpu_custom_call" | custom-call | tf_op jit(solution)/shard_map/pallas_call | solution.py:621

commit v6 on v5

--- a/solution.py
+++ b/solution.py
@@ -307,6 +307,10 @@
     def _(index):
         turn_x(index)
 
+    @pl.loop(1, 4)
+    def _(index):
+        turn_h(index)
+
     others(SLABS, mp, lambda i: kb_copy(i, i).wait_recv())
     kc_copy(core).start()
 
@@ -375,39 +379,6 @@
     def _(a):
         acc_a[a] = grad_a_dot(a, (1, 2, 3))
 
-    @pl.when(mp > 0)
-    def _():
-        x_halo().wait_recv()
-
-    @pl.when(mp == 0)
-    def _():
-        xv[0] = jnp.zeros((64, 2048), BF)
-
-    prepare(0)
-    convolve(0, acc_x)
-    turn_x(0)
-    for rh in range(2):
-        slope(0, rh, bk[rh])
-
-    lane = lax.broadcasted_iota(jnp.int32, (16, 128), 1)
-
-    @pl.loop(0, 3)
-    def _(a):
-        acc = acc_a[a] + grad_a_dot(a, (0,))
-        for b in range(3):
-            this = acc[b * 128 : b * 128 + 128, :128]
-            last = acc[b * 128 + 96 : b * 128 + 128, 128:]
-            turned = pltpu.roll(this, 64, 1)
-            sums = (last + turned[32:64], this[0:32] + turned[64:96], this[32:64] + turned[96:128])
-            for c in range(3):
-                packed = jnp.where(lane < 64, sums[c][:16], pltpu.roll(sums[c][16:], 64, 1))
-                ga_f[pl.ds(pl.multiple_of(a * 144 + b * 48 + c * 16, 16), 16), :] = packed
-
-    ga_f[432:512, :] = jnp.zeros((80, 128), F32)
-    ga_s[...] = ga_f[...].reshape(GROUP, ROWS_A, 128).astype(BF)
-    others(GROUP, me, lambda i: a1_copy(i, me).start())
-    ga_1[me] = ga_s[me]
-
     def grad_b_rows(a, planes, cots):
         lhs = jnp.concatenate(
             [jnp.concatenate([ht[plane, b] for b in range(3)], axis=0) for plane in planes], axis=1
@@ -421,13 +392,44 @@
                 start = a * 72 + b * 24 + c * 8
                 gb_f[:, start : start + 8, :] = pieces[c].reshape(8, 8, 128)
 
-    @pl.loop(0, 4)
-    def _(index):
-        turn_h(index)
-
     grad_b_rows(0, (1, 3), (1, 2))
+    grad_b_rows(2, (1, 3), (0, 1))
+
+    @pl.when(mp > 0)
+    def _():
+        x_halo().wait_recv()
+
+    @pl.when(mp == 0)
+    def _():
+        xv[0] = jnp.zeros((64, 2048), BF)
+
+    prepare(0)
+    convolve(0, acc_x)
+    turn_x(0)
+    for rh in range(2):
+        slope(0, rh, bk[rh])
+
+    lane = lax.broadcasted_iota(jnp.int32, (16, 128), 1)
+
+    @pl.loop(0, 3)
+    def _(a):
+        acc = acc_a[a] + grad_a_dot(a, (0,))
+        for b in range(3):
+            this = acc[b * 128 : b * 128 + 128, :128]
+            last = acc[b * 128 + 96 : b * 128 + 128, 128:]
+            turned = pltpu.roll(this, 64, 1)
+            sums = (last + turned[32:64], this[0:32] + turned[64:96], this[32:64] + turned[96:128])
+            for c in range(3):
+                packed = jnp.where(lane < 64, sums[c][:16], pltpu.roll(sums[c][16:], 64, 1))
+                ga_f[pl.ds(pl.multiple_of(a * 144 + b * 48 + c * 16, 16), 16), :] = packed
+
+    ga_f[432:512, :] = jnp.zeros((80, 128), F32)
+    ga_s[...] = ga_f[...].reshape(GROUP, ROWS_A, 128).astype(BF)
+    others(GROUP, me, lambda i: a1_copy(i, me).start())
+    ga_1[me] = ga_s[me]
+
+    turn_h(0)
     grad_b_rows(1, (0, 2), (0, 1))
-    grad_b_rows(2, (1, 3), (0, 1))
     gb_f[:, 216:224, :] = jnp.zeros((8, 8, 128), F32)
     gb_s[...] = gb_f[:, pl.ds(pl.multiple_of((1 - core) * HALF, 8), HALF), :].astype(BF)
     b0_copy().start()

time: 41.6 us -> 41 us (0.986)
  Pallas kernels: 40.9 us -> 40.3 us
    pallas_call x1, Pallas kernels: 39.7 us -> 39.1 us  [shards(): pl.pallas_call(functools.partial(body, ring, scale_a, scale_b), out_shape...]
where the time goes in v6:
time: 41 us; the launch traced here: 40.9 us
  Pallas kernels  40.3 us (98%)
  between operations  0.64 us (2%)
    pallas_call x1, Pallas kernels, shards(): pl.pallas_call(functools.partial(body, ring, scale_a, scale_b), out_shape...  39.1 us
    pallas_call x1, Pallas kernels, shards(): pl.pallas_call(finish, out_shape=(jax.ShapeDtypeStruct((4096, 16), BF), j...  1.18 us

profile of v6, /device:TPU:1, one launch (start us, length us, event | category | flops | bytes accessed | tf_op | source)
XLA Modules:
  0.0 40.9 jit_solution(11299442485156922470)
XLA Ops:
  0.6 39.1 %shard_map.67 = (bf16[4096,16]{1,0:T(8,128)(2,1)S(1)}, bf16[16,32,128]{2,1,0:T(8,128)(2,1)S(1)}, f32[2,112,128]{2,1,0:T(8,128)S(1)}) custom-call(bf16[8,64,2048]{2,1,0:T(8,128)(2,1)} %bitcast.7, bf16[9,96,64]{2,1,0:T(8,128)(2,1)} %bitcast.11, bf16[216,128]{1,0:T(8,128)(2,1)} %bitcast.13, bf16[4096,16]{1,0:T(8,128)(2,1)} %bitcast.8), custom_call_target="tpu_custom_call" | custom-call | flops 1600000000 | bytes 4000000 | tf_op jit(solution)/shard_map/pallas_call | solution.py:603
  39.7 1.2 %shard_map.68 = (bf16[4096,16]{1,0:T(8,128)(2,1)}, f32[27,32,64]{2,1,0:T(8,128)}, f32[216,128]{1,0:T(8,128)}) custom-call(bf16[4096,16]{1,0:T(8,128)(2,1)S(1)} %get-tuple-element.9.feat_in, bf16[16,32,128]{2,1,0:T(8,128)(2,1)S(1)} %get-tuple-element.10.ga_in, f32[2,112,128]{2,1,0:T(8,128)S(1)} %get-tuple-element.11.gb_in), custom_call_target="tpu_custom_call" | custom-call | tf_op jit(solution)/shard_map/pallas_call | solution.py:623

commit v7 on v6

--- a/solution.py
+++ b/solution.py
@@ -144,6 +144,10 @@
         def _(step):
             act(lax.rem(mine + step, size))
 
+    def each(size, mine, act):
+        for step in range(1, size):
+            act(lax.rem(mine + step, size))
+
     def remote(src, dst, send, recv, device):
         return pltpu.make_async_remote_copy(
             src_ref=src, dst_ref=dst, send_sem=send, recv_sem=recv, device_id=device, device_id_type=MESH
@@ -425,7 +429,7 @@
 
     ga_f[432:512, :] = jnp.zeros((80, 128), F32)
     ga_s[...] = ga_f[...].reshape(GROUP, ROWS_A, 128).astype(BF)
-    others(GROUP, me, lambda i: a1_copy(i, me).start())
+    each(GROUP, me, lambda i: a1_copy(i, me).start())
     ga_1[me] = ga_s[me]
 
     turn_h(0)
@@ -446,7 +450,7 @@
     b0_copy().wait_recv()
     own = pl.ds(pl.multiple_of(core * HALF, 8), HALF)
     gb_h[...] = (gb_f[:, own, :] + gb_0[...].astype(F32)).astype(BF)
-    others(SLABS, mp, lambda i: b1_copy(i, mp).start())
+    each(SLABS, mp, lambda i: b1_copy(i, mp).start())
     gb_1[mp] = gb_h[mp]
     features_of(1, [(1, 0), (2, 1), (3, 2)])
     features_of(2, [(3, 0)])
@@ -455,17 +459,17 @@
 
     others(GROUP, me, lambda i: a1_copy(i, i).wait_recv())
     ga_2s[...] = jnp.sum(ga_1[...].astype(F32), axis=0)
-    others(ring, rank, lambda i: a2_copy(i, rank).start())
+    each(ring, rank, lambda i: a2_copy(i, rank).start())
     ga_2[rank] = ga_2s[...]
 
     others(SLABS, mp, lambda i: b1_copy(i, i).wait_recv())
     gb_2s[...] = jnp.sum(gb_1[...].astype(F32), axis=0).astype(BF)
-    others(ring, rank, lambda i: b2_copy(i, rank).start())
+    each(ring, rank, lambda i: b2_copy(i, rank).start())
     gb_2[rank] = gb_2s[...]
 
     others(ring, rank, lambda i: a2_copy(i, i).wait_recv())
     ga_3s[...] = (jnp.sum(ga_2[...], axis=0) * scale_a).astype(BF)
-    others(GROUP, me, lambda i: a3_copy(i, me).start())
+    each(GROUP, me, lambda i: a3_copy(i, me).start())
     ga_3[me] = ga_3s[...]
 
     others(ring, rank, lambda i: b2_copy(i, i).wait_recv())

time: 41 us -> 40.9 us (level)
  no operation moved by 1% of the time
where the time goes in v7:
time: 40.9 us; the launch traced here: 40.8 us
  Pallas kernels  40.2 us (98%)
  between operations  0.64 us (2%)
    pallas_call x1, Pallas kernels, shards(): pl.pallas_call(functools.partial(body, ring, scale_a, scale_b), out_shape...  39 us
    pallas_call x1, Pallas kernels, shards(): pl.pallas_call(finish, out_shape=(jax.ShapeDtypeStruct((4096, 16), BF), j...  1.18 us

profile of v7, /device:TPU:1, one launch (start us, length us, event | category | flops | bytes accessed | tf_op | source)
XLA Modules:
  0.0 40.8 jit_solution(11375855411978449481)
XLA Ops:
  0.6 39.0 %shard_map.67 = (bf16[4096,16]{1,0:T(8,128)(2,1)S(1)}, bf16[16,32,128]{2,1,0:T(8,128)(2,1)S(1)}, f32[2,112,128]{2,1,0:T(8,128)S(1)}) custom-call(bf16[8,64,2048]{2,1,0:T(8,128)(2,1)} %bitcast.7, bf16[9,96,64]{2,1,0:T(8,128)(2,1)} %bitcast.11, bf16[216,128]{1,0:T(8,128)(2,1)} %bitcast.13, bf16[4096,16]{1,0:T(8,128)(2,1)} %bitcast.8), custom_call_target="tpu_custom_call" | custom-call | flops 1600000000 | bytes 4000000 | tf_op jit(solution)/shard_map/pallas_call | solution.py:607
  39.6 1.2 %shard_map.68 = (bf16[4096,16]{1,0:T(8,128)(2,1)}, f32[27,32,64]{2,1,0:T(8,128)}, f32[216,128]{1,0:T(8,128)}) custom-call(bf16[4096,16]{1,0:T(8,128)(2,1)S(1)} %get-tuple-element.9.feat_in, bf16[16,32,128]{2,1,0:T(8,128)(2,1)S(1)} %get-tuple-element.10.ga_in, f32[2,112,128]{2,1,0:T(8,128)S(1)} %get-tuple-element.11.gb_in), custom_call_target="tpu_custom_call" | custom-call | tf_op jit(solution)/shard_map/pallas_call | solution.py:627
